TPU v7x, 128 devices: a whole 4x4x4 slice. The times are simulated.
128 devices in a mesh: ctx: 8 (over z, x_lo), head: 8 (over y, x_hi), rep: 2 (over core).
Axes of the slice: x: 4 (x_hi: 2, x_lo: 2; x = x_hi * 2 + x_lo), y: 4, z: 4, core: 2. Of those that a mesh axis runs over, the one named last changes fastest.
Arguments:
- prefix_query: bfloat16 [8192, 64, 128], P(('ctx', 'rep'), 'head'), may hold values from -6 to 6
- prefix_kv: bfloat16 [8192, 8, 2, 128], P(('ctx', 'rep'), 'head'), may hold values from -6 to 6
- decode_query: bfloat16 [1024, 64, 128], P(('ctx', 'rep'), 'head'), may hold values from -6 to 6
- tail_key_value: bfloat16 [1024, 128, 8, 2, 128], P(('ctx', 'rep'), None, 'head'), may hold values from -6 to 6
- tail_len: int32 [1024], P(('ctx', 'rep')), may hold values from 1 to 128, as said below
- out_weight: bfloat16 [8192, 8192], P('head', ('ctx', 'rep')), may hold values from -0.0625 to 0.0625
Outputs:
- prefix_out: bfloat16 [8192, 64, 128], P(('ctx', 'rep'), 'head')
- decoded: bfloat16 [1024, 8192], P('head', ('ctx', 'rep'))
Inputs may be any that keep to these rules, and one draw needn't show every extreme that they name: `tail_len`: the last of a rollout's own tokens is its new token; in each aligned block of 64 rollouts some rollout has exactly 128.
All inputs are finite; a program needn't handle non-finite values.
Results may differ from a plain program's by a relative error of at most 0.023.
Values may be sent and summed in bfloat16 or wider, within the bound.
A program may use at most 64 MiB of HBM per device.

v0:
```python
import jax
import jax.numpy as jnp
from jax import lax
from jax.sharding import PartitionSpec as P

LOW_FILL = -1e30


def passed_along(value, axis, by):
    devices = lax.axis_size(axis)
    pairs = [(i, i + by) for i in range(devices) if 0 <= i + by < devices]
    return lax.ppermute(value, axis, pairs)


def shifted(block, axis, distance):
    devices = range(lax.axis_size(axis))
    route = [((i - distance) % len(devices), i) for i in devices]
    return lax.ppermute(block, axis, route)


def absorb(state, scores, visible, values, out_form):
    running_max, running_sum, running_out = state
    if visible is not None:
        scores = jnp.where(visible, scores, LOW_FILL)
    new_max = jnp.maximum(running_max, jnp.max(scores, axis=-1))
    weights = jnp.exp(scores - new_max[..., None])
    if visible is not None:
        weights = jnp.where(visible, weights, 0.0)
    factor = jnp.exp(running_max - new_max)
    running_sum = running_sum * factor + jnp.sum(weights, axis=-1)
    product = jnp.einsum(
        out_form, weights.astype(jnp.bfloat16), values, preferred_element_type=jnp.float32
    )
    running_out = running_out * factor[..., None] + product
    return (new_max, running_sum, running_out)


def with_keys(state, queries, kv_piece, score_scale, visible):
    keys = kv_piece[:, :, 0, :]
    values = kv_piece[:, :, 1, :]
    scores = (
        jnp.einsum("rhgd,thd->rhgt", queries, keys, preferred_element_type=jnp.float32)
        * score_scale
    )
    return absorb(state, scores, visible, values, "rhgt,thd->rhgd")


def fresh_state(row_count, kv_heads, group_width, head_size):
    return (
        jnp.full((row_count, kv_heads, group_width), LOW_FILL, jnp.float32),
        jnp.zeros((row_count, kv_heads, group_width), jnp.float32),
        jnp.zeros((row_count, kv_heads, group_width, head_size), jnp.float32),
    )


def on_device(prefix_query, prefix_kv, decode_query, tail_key_value, tail_len, out_weight):
    cycle_size = lax.axis_size(("ctx", "rep"))
    cycle_place = lax.axis_index(("ctx", "rep"))
    row_count, heads_query, head_size = prefix_query.shape
    kv_heads = prefix_kv.shape[1]
    group_width = heads_query // kv_heads
    roll_count = decode_query.shape[0]
    tail_size = tail_key_value.shape[1]
    score_scale = head_size ** (-0.5)
    queries = prefix_query.reshape(row_count, kv_heads, group_width, head_size)
    roll_query = decode_query.reshape(roll_count, kv_heads, group_width, head_size)
    offsets = jnp.arange(row_count, dtype=jnp.int32)
    diagonal = (offsets[None, :] <= offsets[:, None])[:, None, None, :]
    pre_state = with_keys(
        fresh_state(row_count, kv_heads, group_width, head_size),
        queries,
        prefix_kv,
        score_scale,
        diagonal,
    )
    tail_visible = (jnp.arange(tail_size, dtype=jnp.int32)[None, :] < tail_len[:, None])[
        :, None, None, :
    ]
    tail_scores = (
        jnp.einsum(
            "rhgd,rthd->rhgt",
            roll_query,
            tail_key_value[:, :, :, 0, :],
            preferred_element_type=jnp.float32,
        )
        * score_scale
    )
    roll_state = absorb(
        fresh_state(roll_count, kv_heads, group_width, head_size),
        tail_scores,
        tail_visible,
        tail_key_value[:, :, :, 1, :],
        "rhgt,rthd->rhgd",
    )
    roll_state = with_keys(roll_state, roll_query, prefix_kv, score_scale, None)

    def advance(turn_number, carry):
        kv_piece, state, roll_carry = carry
        kv_piece = passed_along(kv_piece, ("ctx", "rep"), 1)
        source = (cycle_place - turn_number) % cycle_size
        state = lax.cond(
            source < cycle_place,
            lambda current: with_keys(current, queries, kv_piece, score_scale, None),
            lambda current: current,
            state,
        )
        return (kv_piece, state, roll_carry)

    kv_last, pre_state, roll_state = lax.fori_loop(
        1, cycle_size, advance, (prefix_kv, pre_state, roll_state)
    )

    def visit_turn(turn_number, carry):
        visiting, roll_carry = carry
        visiting = shifted(visiting, ("ctx", "rep"), 1)
        roll_carry = shifted((roll_carry[0], roll_carry[1], roll_carry[2]), ("ctx", "rep"), 1)
        roll_carry = with_keys(roll_carry, visiting, prefix_kv, score_scale, None)
        return (visiting, roll_carry)

    visited, roll_state = lax.fori_loop(1, cycle_size, visit_turn, (roll_query, roll_state))
    roll_state = (
        shifted(roll_state[0].astype(jnp.bfloat16), ("ctx", "rep"), 1).astype(jnp.float32),
        shifted(roll_state[1].astype(jnp.bfloat16), ("ctx", "rep"), 1).astype(jnp.float32),
        shifted(roll_state[2].astype(jnp.bfloat16), ("ctx", "rep"), 1).astype(jnp.float32),
    )
    prefix_out = (
        (pre_state[2] / pre_state[1][..., None])
        .astype(jnp.bfloat16)
        .reshape(row_count, heads_query, head_size)
    )
    attended = (
        (roll_state[2] / roll_state[1][..., None])
        .astype(jnp.bfloat16)
        .reshape(roll_count, heads_query * head_size)
    )
    partial_terms = jnp.dot(
        lax.all_gather(attended, ("ctx", "rep"), axis=0, tiled=True),
        out_weight,
        preferred_element_type=jnp.float32,
    )
    decoded = lax.psum_scatter(
        partial_terms.astype(jnp.bfloat16), "head", scatter_dimension=0, tiled=True
    )
    return (prefix_out, decoded)


def solution(mesh):
    return jax.shard_map(
        on_device,
        mesh=mesh,
        in_specs=(
            P(("ctx", "rep"), "head", None),
            P(("ctx", "rep"), "head", None, None),
            P(("ctx", "rep"), "head", None),
            P(("ctx", "rep"), None, "head", None, None),
            P(("ctx", "rep")),
            P("head", ("ctx", "rep")),
        ),
        out_specs=(P(("ctx", "rep"), "head", None), P("head", ("ctx", "rep"))),
        check_vma=False,
    )
```

profile of v0, /device:TPU:99, one launch (start us, length us, event | category | flops | bytes accessed | tf_op | source)
XLA Modules:
  0.0 479.0 jit_solution(510210245706295814)
XLA Ops:
  12.0 9.8 %fusion.78 = (bf16[64,128,1,1,128]{4,3,2,1,0:T(2,128)(2,1)}, bf16[64,128,1,1,128]{4,3,2,1,0:T(2,128)(2,1)S(1)}) fusion(bf16[64,128,1,2,128]{4,3,2,1,0:T(2,128)(2,1)} %param.15), kind=kLoop, calls=%fused_computation.111 | loop fusion | bytes 8388608 | tf_op jit(solution)/shard_map/slice | solution.py:92
  24.0 2.9 fusion.51
  28.3 157.6 %while.38 = (s32[]{:T(128)}, bf16[64,1,8,128]{3,0,2,1:T(8,128)(2,1)S(1)}, f32[64,1,8]{0,2,1:T(8,128)S(1)}, f32[64,1,8]{0,2,1:T(8,128)S(1)}, f32[64,1,8,128]{3,2,...) while((s32[]{:T(128)}, bf16[64,1,8,128]{3,0,2,1:T(8,128)(2,1)S(1)}, ...), condition=%wide.region_15.16_spmd, body=%wide.region_12.15_spmd.sunk | while | flops 135661056 | bytes 5945581 | solution.py:120
  34.5 4.7 collective-permute-start.1
  45.3 4.7 collective-permute-start.1
  56.2 4.7 collective-permute-start.1
  67.0 4.7 collective-permute-start.1
  77.8 4.7 collective-permute-start.1
  88.6 4.7 collective-permute-start.1
  99.4 4.7 collective-permute-start.1
  110.2 4.7 collective-permute-start.1
  121.0 4.7 collective-permute-start.1
  131.8 4.7 collective-permute-start.1
  142.6 4.7 collective-permute-start.1
  153.4 4.7 collective-permute-start.1
  164.3 4.7 collective-permute-start.1
  175.1 4.7 collective-permute-start.1
  185.9 4.7 collective-permute-start.6
  194.9 5.7 %fusion.33 = (f32[512,8]{0,1:T(8,128)S(1)}, f32[512,512,8]{1,0,2:T(8,128)}) fusion(pred[512,512]{0,1:T(8,128)(4,1)S(1)} %iota_compare_fusion, bf16[512,8,128]{2,1,0:T(8,128)(2,1)S(1)} %copy-done.1, bf16[512,1,2,128]{3,0,2,1:T(8,128)(2,1)} %copy.82), kind=kOutput, calls=%fused_computation.41 | convolution fusion | flops 543158272 | bytes 9846784 | tf_op jit(solution)/shard_map/rhgd,thd->rhgt/dot_general | solution.py:42
  200.6 28.4 %all-gather.2.cloned.1.call-done = bf16[1024,1024]{1,0:T(8,128)(2,1)} async-done(((bf16[64,1024]{1,0:T(8,128)(2,1)}), bf16[1024,1024]{1,0:T(8,128)(2,1)}) %all-gather.2.cloned.1.call-update) | async-done | bytes 2097168 | tf_op jit(solution)/shard_map/all_gather | solution.py:137
  229.0 3.8 convolution_convert_fusion
  232.8 4.5 fusion.35
  237.3 5.0 %fusion.42 = f32[512,1,8,128]{3,0,2,1:T(8,128)S(1)} fusion(f32[512,512,8]{1,0,2:T(8,128)} %get-tuple-element.358, f32[512,8]{0,1:T(8,128)S(1)} %get-tuple-element.350, pred[512,512]{0,1:T(8,128)(4,1)S(1)} %iota_compare_fusion, f32[512,8]{0,1:T(8,128)S(1)} %get-tuple-element.348, bf16[512,1,2,128]{3,0,2,1:T(8,128)(2,1)} %copy.82), kind=kOutput, calls=%fused_computation.52 | convolution fusion | flops 547880960 | bytes 10911744 | tf_op jit(solution)/shard_map/rhgt,thd->rhgd/dot_general | solution.py:31
  242.4 226.0 %while.37 = (s32[]{:T(128)}, bf16[512,1,2,128]{3,0,2,1:T(8,128)(2,1)}, f32[512,1,8]{0,2,1:T(8,128)S(1)}, f32[512,1,8]{0,2,1:T(8,128)S(1)}, f32[512,1,8,128]{3,0,...) while((s32[]{:T(128)}, ...), condition=%wide.region_7.8_spmd, body=%wide.region_2.7_spmd.sunk | while | flops 1091579904 | bytes 32506236 | solution.py:109
  246.0 6.4 %conditional.2 = ((f32[512,1,8]{0,2,1:T(8,128)S(1)}, f32[512,1,8]{0,2,1:T(8,128)S(1)}, f32[512,1,8,128]{3,0,2,1:T(8,128)S(1)})) conditional(s32[]{:T(128)} %convert_element_type.82, (f32[512,1,8]{0,2,1:T(8,128)S(1)}, f32[512,1,8]{0,2,1:T(8,128)S(1)}, f32[512,1,8,128]{3,0,2,1:T(8,128)S(1)}) %tuple.88, (bf16[512,1,2,128]{3,0,2,1:T(8,128)(2,1)S(1)}, ...), branch_computations={%region_3.3_spmd, %region_4.6_spmd} | conditional | flops 1091579904 | bytes 30933024 | solution.py:101
  246.0 2.5 bitcast_reduce_fusion
  254.4 6.3 %collective-permute-done = bf16[512,1,2,128]{3,0,2,1:T(8,128)(2,1)S(1)} collective-permute-done((bf16[512,1,2,128]{3,0,2,1:T(8,128)(2,1)}, bf16[512,1,2,128]{3,0,2,1:T(8,128)(2,1)S(1)}, u32[]{:S(2)}, u32[]{:S(2)}) %collective-permute-start) | collective-permute-done | bytes 262176 | tf_op jit(solution)/shard_map/while/body/eval_jaxpr/ppermute | solution.py:12
  260.8 6.4 %conditional.2 = ((f32[512,1,8]{0,2,1:T(8,128)S(1)}, f32[512,1,8]{0,2,1:T(8,128)S(1)}, f32[512,1,8,128]{3,0,2,1:T(8,128)S(1)})) conditional(s32[]{:T(128)} %convert_element_type.82, (f32[512,1,8]{0,2,1:T(8,128)S(1)}, f32[512,1,8]{0,2,1:T(8,128)S(1)}, f32[512,1,8,128]{3,0,2,1:T(8,128)S(1)}) %tuple.88, (bf16[512,1,2,128]{3,0,2,1:T(8,128)(2,1)S(1)}, ...), branch_computations={%region_3.3_spmd, %region_4.6_spmd} | conditional | flops 1091579904 | bytes 30933024 | solution.py:101
  260.8 2.5 bitcast_reduce_fusion
  269.2 7.0 %collective-permute-done = bf16[512,1,2,128]{3,0,2,1:T(8,128)(2,1)S(1)} collective-permute-done((bf16[512,1,2,128]{3,0,2,1:T(8,128)(2,1)}, bf16[512,1,2,128]{3,0,2,1:T(8,128)(2,1)S(1)}, u32[]{:S(2)}, u32[]{:S(2)}) %collective-permute-start) | collective-permute-done | bytes 262176 | tf_op jit(solution)/shard_map/while/body/eval_jaxpr/ppermute | solution.py:12
  276.1 6.4 %conditional.2 = ((f32[512,1,8]{0,2,1:T(8,128)S(1)}, f32[512,1,8]{0,2,1:T(8,128)S(1)}, f32[512,1,8,128]{3,0,2,1:T(8,128)S(1)})) conditional(s32[]{:T(128)} %convert_element_type.82, (f32[512,1,8]{0,2,1:T(8,128)S(1)}, f32[512,1,8]{0,2,1:T(8,128)S(1)}, f32[512,1,8,128]{3,0,2,1:T(8,128)S(1)}) %tuple.88, (bf16[512,1,2,128]{3,0,2,1:T(8,128)(2,1)S(1)}, ...), branch_computations={%region_3.3_spmd, %region_4.6_spmd} | conditional | flops 1091579904 | bytes 30933024 | solution.py:101
  276.1 2.5 bitcast_reduce_fusion
  284.5 7.1 %collective-permute-done = bf16[512,1,2,128]{3,0,2,1:T(8,128)(2,1)S(1)} collective-permute-done((bf16[512,1,2,128]{3,0,2,1:T(8,128)(2,1)}, bf16[512,1,2,128]{3,0,2,1:T(8,128)(2,1)S(1)}, u32[]{:S(2)}, u32[]{:S(2)}) %collective-permute-start) | collective-permute-done | bytes 262176 | tf_op jit(solution)/shard_map/while/body/eval_jaxpr/ppermute | solution.py:12
  291.6 6.4 %conditional.2 = ((f32[512,1,8]{0,2,1:T(8,128)S(1)}, f32[512,1,8]{0,2,1:T(8,128)S(1)}, f32[512,1,8,128]{3,0,2,1:T(8,128)S(1)})) conditional(s32[]{:T(128)} %convert_element_type.82, (f32[512,1,8]{0,2,1:T(8,128)S(1)}, f32[512,1,8]{0,2,1:T(8,128)S(1)}, f32[512,1,8,128]{3,0,2,1:T(8,128)S(1)}) %tuple.88, (bf16[512,1,2,128]{3,0,2,1:T(8,128)(2,1)S(1)}, ...), branch_computations={%region_3.3_spmd, %region_4.6_spmd} | conditional | flops 1091579904 | bytes 30933024 | solution.py:101
  291.6 2.5 bitcast_reduce_fusion
  300.0 8.0 %collective-permute-done = bf16[512,1,2,128]{3,0,2,1:T(8,128)(2,1)S(1)} collective-permute-done((bf16[512,1,2,128]{3,0,2,1:T(8,128)(2,1)}, bf16[512,1,2,128]{3,0,2,1:T(8,128)(2,1)S(1)}, u32[]{:S(2)}, u32[]{:S(2)}) %collective-permute-start) | collective-permute-done | bytes 262176 | tf_op jit(solution)/shard_map/while/body/eval_jaxpr/ppermute | solution.py:12
  308.0 6.4 %conditional.2 = ((f32[512,1,8]{0,2,1:T(8,128)S(1)}, f32[512,1,8]{0,2,1:T(8,128)S(1)}, f32[512,1,8,128]{3,0,2,1:T(8,128)S(1)})) conditional(s32[]{:T(128)} %convert_element_type.82, (f32[512,1,8]{0,2,1:T(8,128)S(1)}, f32[512,1,8]{0,2,1:T(8,128)S(1)}, f32[512,1,8,128]{3,0,2,1:T(8,128)S(1)}) %tuple.88, (bf16[512,1,2,128]{3,0,2,1:T(8,128)(2,1)S(1)}, ...), branch_computations={%region_3.3_spmd, %region_4.6_spmd} | conditional | flops 1091579904 | bytes 30933024 | solution.py:101
  308.0 2.5 bitcast_reduce_fusion
  316.4 6.6 %collective-permute-done = bf16[512,1,2,128]{3,0,2,1:T(8,128)(2,1)S(1)} collective-permute-done((bf16[512,1,2,128]{3,0,2,1:T(8,128)(2,1)}, bf16[512,1,2,128]{3,0,2,1:T(8,128)(2,1)S(1)}, u32[]{:S(2)}, u32[]{:S(2)}) %collective-permute-start) | collective-permute-done | bytes 262176 | tf_op jit(solution)/shard_map/while/body/eval_jaxpr/ppermute | solution.py:12
  323.0 6.4 %conditional.2 = ((f32[512,1,8]{0,2,1:T(8,128)S(1)}, f32[512,1,8]{0,2,1:T(8,128)S(1)}, f32[512,1,8,128]{3,0,2,1:T(8,128)S(1)})) conditional(s32[]{:T(128)} %convert_element_type.82, (f32[512,1,8]{0,2,1:T(8,128)S(1)}, f32[512,1,8]{0,2,1:T(8,128)S(1)}, f32[512,1,8,128]{3,0,2,1:T(8,128)S(1)}) %tuple.88, (bf16[512,1,2,128]{3,0,2,1:T(8,128)(2,1)S(1)}, ...), branch_computations={%region_3.3_spmd, %region_4.6_spmd} | conditional | flops 1091579904 | bytes 30933024 | solution.py:101
  331.3 6.6 %collective-permute-done = bf16[512,1,2,128]{3,0,2,1:T(8,128)(2,1)S(1)} collective-permute-done((bf16[512,1,2,128]{3,0,2,1:T(8,128)(2,1)}, bf16[512,1,2,128]{3,0,2,1:T(8,128)(2,1)S(1)}, u32[]{:S(2)}, u32[]{:S(2)}) %collective-permute-start) | collective-permute-done | bytes 262176 | tf_op jit(solution)/shard_map/while/body/eval_jaxpr/ppermute | solution.py:12
  337.9 6.4 %conditional.2 = ((f32[512,1,8]{0,2,1:T(8,128)S(1)}, f32[512,1,8]{0,2,1:T(8,128)S(1)}, f32[512,1,8,128]{3,0,2,1:T(8,128)S(1)})) conditional(s32[]{:T(128)} %convert_element_type.82, (f32[512,1,8]{0,2,1:T(8,128)S(1)}, f32[512,1,8]{0,2,1:T(8,128)S(1)}, f32[512,1,8,128]{3,0,2,1:T(8,128)S(1)}) %tuple.88, (bf16[512,1,2,128]{3,0,2,1:T(8,128)(2,1)S(1)}, ...), branch_computations={%region_3.3_spmd, %region_4.6_spmd} | conditional | flops 1091579904 | bytes 30933024 | solution.py:101
  337.9 2.5 bitcast_reduce_fusion
  346.3 6.6 %collective-permute-done = bf16[512,1,2,128]{3,0,2,1:T(8,128)(2,1)S(1)} collective-permute-done((bf16[512,1,2,128]{3,0,2,1:T(8,128)(2,1)}, bf16[512,1,2,128]{3,0,2,1:T(8,128)(2,1)S(1)}, u32[]{:S(2)}, u32[]{:S(2)}) %collective-permute-start) | collective-permute-done | bytes 262176 | tf_op jit(solution)/shard_map/while/body/eval_jaxpr/ppermute | solution.py:12
  352.9 6.4 %conditional.2 = ((f32[512,1,8]{0,2,1:T(8,128)S(1)}, f32[512,1,8]{0,2,1:T(8,128)S(1)}, f32[512,1,8,128]{3,0,2,1:T(8,128)S(1)})) conditional(s32[]{:T(128)} %convert_element_type.82, (f32[512,1,8]{0,2,1:T(8,128)S(1)}, f32[512,1,8]{0,2,1:T(8,128)S(1)}, f32[512,1,8,128]{3,0,2,1:T(8,128)S(1)}) %tuple.88, (bf16[512,1,2,128]{3,0,2,1:T(8,128)(2,1)S(1)}, ...), branch_computations={%region_3.3_spmd, %region_4.6_spmd} | conditional | flops 1091579904 | bytes 30933024 | solution.py:101
  352.9 2.5 bitcast_reduce_fusion
  361.3 6.6 %collective-permute-done = bf16[512,1,2,128]{3,0,2,1:T(8,128)(2,1)S(1)} collective-permute-done((bf16[512,1,2,128]{3,0,2,1:T(8,128)(2,1)}, bf16[512,1,2,128]{3,0,2,1:T(8,128)(2,1)S(1)}, u32[]{:S(2)}, u32[]{:S(2)}) %collective-permute-start) | collective-permute-done | bytes 262176 | tf_op jit(solution)/shard_map/while/body/eval_jaxpr/ppermute | solution.py:12
  367.8 6.4 %conditional.2 = ((f32[512,1,8]{0,2,1:T(8,128)S(1)}, f32[512,1,8]{0,2,1:T(8,128)S(1)}, f32[512,1,8,128]{3,0,2,1:T(8,128)S(1)})) conditional(s32[]{:T(128)} %convert_element_type.82, (f32[512,1,8]{0,2,1:T(8,128)S(1)}, f32[512,1,8]{0,2,1:T(8,128)S(1)}, f32[512,1,8,128]{3,0,2,1:T(8,128)S(1)}) %tuple.88, (bf16[512,1,2,128]{3,0,2,1:T(8,128)(2,1)S(1)}, ...), branch_computations={%region_3.3_spmd, %region_4.6_spmd} | conditional | flops 1091579904 | bytes 30933024 | solution.py:101
  367.8 2.5 bitcast_reduce_fusion
  376.2 6.6 %collective-permute-done = bf16[512,1,2,128]{3,0,2,1:T(8,128)(2,1)S(1)} collective-permute-done((bf16[512,1,2,128]{3,0,2,1:T(8,128)(2,1)}, bf16[512,1,2,128]{3,0,2,1:T(8,128)(2,1)S(1)}, u32[]{:S(2)}, u32[]{:S(2)}) %collective-permute-start) | collective-permute-done | bytes 262176 | tf_op jit(solution)/shard_map/while/body/eval_jaxpr/ppermute | solution.py:12
  382.8 6.4 %conditional.2 = ((f32[512,1,8]{0,2,1:T(8,128)S(1)}, f32[512,1,8]{0,2,1:T(8,128)S(1)}, f32[512,1,8,128]{3,0,2,1:T(8,128)S(1)})) conditional(s32[]{:T(128)} %convert_element_type.82, (f32[512,1,8]{0,2,1:T(8,128)S(1)}, f32[512,1,8]{0,2,1:T(8,128)S(1)}, f32[512,1,8,128]{3,0,2,1:T(8,128)S(1)}) %tuple.88, (bf16[512,1,2,128]{3,0,2,1:T(8,128)(2,1)S(1)}, ...), branch_computations={%region_3.3_spmd, %region_4.6_spmd} | conditional | flops 1091579904 | bytes 30933024 | solution.py:101
  382.8 2.5 bitcast_reduce_fusion
  391.2 6.7 %collective-permute-done = bf16[512,1,2,128]{3,0,2,1:T(8,128)(2,1)S(1)} collective-permute-done((bf16[512,1,2,128]{3,0,2,1:T(8,128)(2,1)}, bf16[512,1,2,128]{3,0,2,1:T(8,128)(2,1)S(1)}, u32[]{:S(2)}, u32[]{:S(2)}) %collective-permute-start) | collective-permute-done | bytes 262176 | tf_op jit(solution)/shard_map/while/body/eval_jaxpr/ppermute | solution.py:12
  397.9 6.4 %conditional.2 = ((f32[512,1,8]{0,2,1:T(8,128)S(1)}, f32[512,1,8]{0,2,1:T(8,128)S(1)}, f32[512,1,8,128]{3,0,2,1:T(8,128)S(1)})) conditional(s32[]{:T(128)} %convert_element_type.82, (f32[512,1,8]{0,2,1:T(8,128)S(1)}, f32[512,1,8]{0,2,1:T(8,128)S(1)}, f32[512,1,8,128]{3,0,2,1:T(8,128)S(1)}) %tuple.88, (bf16[512,1,2,128]{3,0,2,1:T(8,128)(2,1)S(1)}, ...), branch_computations={%region_3.3_spmd, %region_4.6_spmd} | conditional | flops 1091579904 | bytes 30933024 | solution.py:101
  397.9 2.5 bitcast_reduce_fusion
  406.3 7.5 %collective-permute-done = bf16[512,1,2,128]{3,0,2,1:T(8,128)(2,1)S(1)} collective-permute-done((bf16[512,1,2,128]{3,0,2,1:T(8,128)(2,1)}, bf16[512,1,2,128]{3,0,2,1:T(8,128)(2,1)S(1)}, u32[]{:S(2)}, u32[]{:S(2)}) %collective-permute-start) | collective-permute-done | bytes 262176 | tf_op jit(solution)/shard_map/while/body/eval_jaxpr/ppermute | solution.py:12
  413.8 6.4 %conditional.2 = ((f32[512,1,8]{0,2,1:T(8,128)S(1)}, f32[512,1,8]{0,2,1:T(8,128)S(1)}, f32[512,1,8,128]{3,0,2,1:T(8,128)S(1)})) conditional(s32[]{:T(128)} %convert_element_type.82, (f32[512,1,8]{0,2,1:T(8,128)S(1)}, f32[512,1,8]{0,2,1:T(8,128)S(1)}, f32[512,1,8,128]{3,0,2,1:T(8,128)S(1)}) %tuple.88, (bf16[512,1,2,128]{3,0,2,1:T(8,128)(2,1)S(1)}, ...), branch_computations={%region_3.3_spmd, %region_4.6_spmd} | conditional | flops 1091579904 | bytes 30933024 | solution.py:101
  422.2 7.5 %collective-permute-done = bf16[512,1,2,128]{3,0,2,1:T(8,128)(2,1)S(1)} collective-permute-done((bf16[512,1,2,128]{3,0,2,1:T(8,128)(2,1)}, bf16[512,1,2,128]{3,0,2,1:T(8,128)(2,1)S(1)}, u32[]{:S(2)}, u32[]{:S(2)}) %collective-permute-start) | collective-permute-done | bytes 262176 | tf_op jit(solution)/shard_map/while/body/eval_jaxpr/ppermute | solution.py:12
  429.6 6.4 %conditional.2 = ((f32[512,1,8]{0,2,1:T(8,128)S(1)}, f32[512,1,8]{0,2,1:T(8,128)S(1)}, f32[512,1,8,128]{3,0,2,1:T(8,128)S(1)})) conditional(s32[]{:T(128)} %convert_element_type.82, (f32[512,1,8]{0,2,1:T(8,128)S(1)}, f32[512,1,8]{0,2,1:T(8,128)S(1)}, f32[512,1,8,128]{3,0,2,1:T(8,128)S(1)}) %tuple.88, (bf16[512,1,2,128]{3,0,2,1:T(8,128)(2,1)S(1)}, ...), branch_computations={%region_3.3_spmd, %region_4.6_spmd} | conditional | flops 1091579904 | bytes 30933024 | solution.py:101
  438.0 7.5 %collective-permute-done = bf16[512,1,2,128]{3,0,2,1:T(8,128)(2,1)S(1)} collective-permute-done((bf16[512,1,2,128]{3,0,2,1:T(8,128)(2,1)}, bf16[512,1,2,128]{3,0,2,1:T(8,128)(2,1)S(1)}, u32[]{:S(2)}, u32[]{:S(2)}) %collective-permute-start) | collective-permute-done | bytes 262176 | tf_op jit(solution)/shard_map/while/body/eval_jaxpr/ppermute | solution.py:12
  445.5 6.4 %conditional.2 = ((f32[512,1,8]{0,2,1:T(8,128)S(1)}, f32[512,1,8]{0,2,1:T(8,128)S(1)}, f32[512,1,8,128]{3,0,2,1:T(8,128)S(1)})) conditional(s32[]{:T(128)} %convert_element_type.82, (f32[512,1,8]{0,2,1:T(8,128)S(1)}, f32[512,1,8]{0,2,1:T(8,128)S(1)}, f32[512,1,8,128]{3,0,2,1:T(8,128)S(1)}) %tuple.88, (bf16[512,1,2,128]{3,0,2,1:T(8,128)(2,1)S(1)}, ...), branch_computations={%region_3.3_spmd, %region_4.6_spmd} | conditional | flops 1091579904 | bytes 30933024 | solution.py:101
  453.9 7.5 %collective-permute-done = bf16[512,1,2,128]{3,0,2,1:T(8,128)(2,1)S(1)} collective-permute-done((bf16[512,1,2,128]{3,0,2,1:T(8,128)(2,1)}, bf16[512,1,2,128]{3,0,2,1:T(8,128)(2,1)S(1)}, u32[]{:S(2)}, u32[]{:S(2)}) %collective-permute-start) | collective-permute-done | bytes 262176 | tf_op jit(solution)/shard_map/while/body/eval_jaxpr/ppermute | solution.py:12
  461.3 6.4 %conditional.2 = ((f32[512,1,8]{0,2,1:T(8,128)S(1)}, f32[512,1,8]{0,2,1:T(8,128)S(1)}, f32[512,1,8,128]{3,0,2,1:T(8,128)S(1)})) conditional(s32[]{:T(128)} %convert_element_type.82, (f32[512,1,8]{0,2,1:T(8,128)S(1)}, f32[512,1,8]{0,2,1:T(8,128)S(1)}, f32[512,1,8,128]{3,0,2,1:T(8,128)S(1)}) %tuple.88, (bf16[512,1,2,128]{3,0,2,1:T(8,128)(2,1)S(1)}, ...), branch_computations={%region_3.3_spmd, %region_4.6_spmd} | conditional | flops 1091579904 | bytes 30933024 | solution.py:101
  468.5 3.6 fusion.53
  (362 shorter events, 206.2 us)
Async XLA Ops:
  7.2 221.8 %all-gather.2.cloned.1.call-start = ((), (), s32[]{:S(2)}) async-start(), calls=%async_computation.1 | async-start | bytes 2228224 | tf_op jit(solution)/shard_map/all_gather | solution.py:137
  28.5 3.6 collective-permute-start.3
  29.4 3.8 collective-permute-start.4
  34.5 6.6 %collective-permute-start.1 = (bf16[64,1,8,128]{3,0,2,1:T(8,128)(2,1)S(1)}, bf16[64,1,8,128]{3,0,2,1:T(8,128)(2,1)S(1)}, u32[]{:S(2)}, u32[]{:S(2)}) collective-permute-start(bf16[64,1,8,128]{3,0,2,1:T(8,128)(2,1)S(1)} %get-tuple-element.508), channel_id=1, source_target_pairs={{113,0},{0,1},{1,16},{16,17},{17,32},{32,33},{33,48},{48,49},{49,6... | collective-permute-start | bytes 393224 | tf_op jit(solution)/shard_map/while/body/eval_jaxpr/ppermute | solution.py:18
  39.3 3.6 collective-permute-start.3
  39.4 4.6 collective-permute-start.4
  45.3 6.6 %collective-permute-start.1 = (bf16[64,1,8,128]{3,0,2,1:T(8,128)(2,1)S(1)}, bf16[64,1,8,128]{3,0,2,1:T(8,128)(2,1)S(1)}, u32[]{:S(2)}, u32[]{:S(2)}) collective-permute-start(bf16[64,1,8,128]{3,0,2,1:T(8,128)(2,1)S(1)} %get-tuple-element.508), channel_id=1, source_target_pairs={{113,0},{0,1},{1,16},{16,17},{17,32},{32,33},{33,48},{48,49},{49,6... | collective-permute-start | bytes 393224 | tf_op jit(solution)/shard_map/while/body/eval_jaxpr/ppermute | solution.py:18
  50.0 3.2 collective-permute-start.2
  50.1 3.6 collective-permute-start.3
  50.2 4.6 collective-permute-start.4
  56.2 6.6 %collective-permute-start.1 = (bf16[64,1,8,128]{3,0,2,1:T(8,128)(2,1)S(1)}, bf16[64,1,8,128]{3,0,2,1:T(8,128)(2,1)S(1)}, u32[]{:S(2)}, u32[]{:S(2)}) collective-permute-start(bf16[64,1,8,128]{3,0,2,1:T(8,128)(2,1)S(1)} %get-tuple-element.508), channel_id=1, source_target_pairs={{113,0},{0,1},{1,16},{16,17},{17,32},{32,33},{33,48},{48,49},{49,6... | collective-permute-start | bytes 393224 | tf_op jit(solution)/shard_map/while/body/eval_jaxpr/ppermute | solution.py:18
  60.9 3.6 collective-permute-start.3
  61.0 4.6 collective-permute-start.4
  67.0 6.6 %collective-permute-start.1 = (bf16[64,1,8,128]{3,0,2,1:T(8,128)(2,1)S(1)}, bf16[64,1,8,128]{3,0,2,1:T(8,128)(2,1)S(1)}, u32[]{:S(2)}, u32[]{:S(2)}) collective-permute-start(bf16[64,1,8,128]{3,0,2,1:T(8,128)(2,1)S(1)} %get-tuple-element.508), channel_id=1, source_target_pairs={{113,0},{0,1},{1,16},{16,17},{17,32},{32,33},{33,48},{48,49},{49,6... | collective-permute-start | bytes 393224 | tf_op jit(solution)/shard_map/while/body/eval_jaxpr/ppermute | solution.py:18
  71.7 3.6 collective-permute-start.3
  71.8 4.6 collective-permute-start.4
  77.8 6.6 %collective-permute-start.1 = (bf16[64,1,8,128]{3,0,2,1:T(8,128)(2,1)S(1)}, bf16[64,1,8,128]{3,0,2,1:T(8,128)(2,1)S(1)}, u32[]{:S(2)}, u32[]{:S(2)}) collective-permute-start(bf16[64,1,8,128]{3,0,2,1:T(8,128)(2,1)S(1)} %get-tuple-element.508), channel_id=1, source_target_pairs={{113,0},{0,1},{1,16},{16,17},{17,32},{32,33},{33,48},{48,49},{49,6... | collective-permute-start | bytes 393224 | tf_op jit(solution)/shard_map/while/body/eval_jaxpr/ppermute | solution.py:18
  82.4 3.2 collective-permute-start.2
  82.5 3.6 collective-permute-start.3
  82.6 4.6 collective-permute-start.4
  88.6 6.6 %collective-permute-start.1 = (bf16[64,1,8,128]{3,0,2,1:T(8,128)(2,1)S(1)}, bf16[64,1,8,128]{3,0,2,1:T(8,128)(2,1)S(1)}, u32[]{:S(2)}, u32[]{:S(2)}) collective-permute-start(bf16[64,1,8,128]{3,0,2,1:T(8,128)(2,1)S(1)} %get-tuple-element.508), channel_id=1, source_target_pairs={{113,0},{0,1},{1,16},{16,17},{17,32},{32,33},{33,48},{48,49},{49,6... | collective-permute-start | bytes 393224 | tf_op jit(solution)/shard_map/while/body/eval_jaxpr/ppermute | solution.py:18
  93.3 3.6 collective-permute-start.3
  93.4 4.6 collective-permute-start.4
  99.4 6.6 %collective-permute-start.1 = (bf16[64,1,8,128]{3,0,2,1:T(8,128)(2,1)S(1)}, bf16[64,1,8,128]{3,0,2,1:T(8,128)(2,1)S(1)}, u32[]{:S(2)}, u32[]{:S(2)}) collective-permute-start(bf16[64,1,8,128]{3,0,2,1:T(8,128)(2,1)S(1)} %get-tuple-element.508), channel_id=1, source_target_pairs={{113,0},{0,1},{1,16},{16,17},{17,32},{32,33},{33,48},{48,49},{49,6... | collective-permute-start | bytes 393224 | tf_op jit(solution)/shard_map/while/body/eval_jaxpr/ppermute | solution.py:18
  104.1 3.6 collective-permute-start.3
  104.2 4.6 collective-permute-start.4
  110.2 6.6 %collective-permute-start.1 = (bf16[64,1,8,128]{3,0,2,1:T(8,128)(2,1)S(1)}, bf16[64,1,8,128]{3,0,2,1:T(8,128)(2,1)S(1)}, u32[]{:S(2)}, u32[]{:S(2)}) collective-permute-start(bf16[64,1,8,128]{3,0,2,1:T(8,128)(2,1)S(1)} %get-tuple-element.508), channel_id=1, source_target_pairs={{113,0},{0,1},{1,16},{16,17},{17,32},{32,33},{33,48},{48,49},{49,6... | collective-permute-start | bytes 393224 | tf_op jit(solution)/shard_map/while/body/eval_jaxpr/ppermute | solution.py:18
  114.9 3.6 collective-permute-start.3
  115.0 4.6 collective-permute-start.4
  121.0 6.6 %collective-permute-start.1 = (bf16[64,1,8,128]{3,0,2,1:T(8,128)(2,1)S(1)}, bf16[64,1,8,128]{3,0,2,1:T(8,128)(2,1)S(1)}, u32[]{:S(2)}, u32[]{:S(2)}) collective-permute-start(bf16[64,1,8,128]{3,0,2,1:T(8,128)(2,1)S(1)} %get-tuple-element.508), channel_id=1, source_target_pairs={{113,0},{0,1},{1,16},{16,17},{17,32},{32,33},{33,48},{48,49},{49,6... | collective-permute-start | bytes 393224 | tf_op jit(solution)/shard_map/while/body/eval_jaxpr/ppermute | solution.py:18
  125.8 3.6 collective-permute-start.3
  125.8 4.6 collective-permute-start.4
  131.8 6.6 %collective-permute-start.1 = (bf16[64,1,8,128]{3,0,2,1:T(8,128)(2,1)S(1)}, bf16[64,1,8,128]{3,0,2,1:T(8,128)(2,1)S(1)}, u32[]{:S(2)}, u32[]{:S(2)}) collective-permute-start(bf16[64,1,8,128]{3,0,2,1:T(8,128)(2,1)S(1)} %get-tuple-element.508), channel_id=1, source_target_pairs={{113,0},{0,1},{1,16},{16,17},{17,32},{32,33},{33,48},{48,49},{49,6... | collective-permute-start | bytes 393224 | tf_op jit(solution)/shard_map/while/body/eval_jaxpr/ppermute | solution.py:18
  136.6 3.6 collective-permute-start.3
  136.6 4.6 collective-permute-start.4
  142.6 6.6 %collective-permute-start.1 = (bf16[64,1,8,128]{3,0,2,1:T(8,128)(2,1)S(1)}, bf16[64,1,8,128]{3,0,2,1:T(8,128)(2,1)S(1)}, u32[]{:S(2)}, u32[]{:S(2)}) collective-permute-start(bf16[64,1,8,128]{3,0,2,1:T(8,128)(2,1)S(1)} %get-tuple-element.508), channel_id=1, source_target_pairs={{113,0},{0,1},{1,16},{16,17},{17,32},{32,33},{33,48},{48,49},{49,6... | collective-permute-start | bytes 393224 | tf_op jit(solution)/shard_map/while/body/eval_jaxpr/ppermute | solution.py:18
  147.4 3.6 collective-permute-start.3
  147.5 4.6 collective-permute-start.4
  153.4 6.6 %collective-permute-start.1 = (bf16[64,1,8,128]{3,0,2,1:T(8,128)(2,1)S(1)}, bf16[64,1,8,128]{3,0,2,1:T(8,128)(2,1)S(1)}, u32[]{:S(2)}, u32[]{:S(2)}) collective-permute-start(bf16[64,1,8,128]{3,0,2,1:T(8,128)(2,1)S(1)} %get-tuple-element.508), channel_id=1, source_target_pairs={{113,0},{0,1},{1,16},{16,17},{17,32},{32,33},{33,48},{48,49},{49,6... | collective-permute-start | bytes 393224 | tf_op jit(solution)/shard_map/while/body/eval_jaxpr/ppermute | solution.py:18
  158.2 3.6 collective-permute-start.3
  158.3 4.6 collective-permute-start.4
  164.3 6.6 %collective-permute-start.1 = (bf16[64,1,8,128]{3,0,2,1:T(8,128)(2,1)S(1)}, bf16[64,1,8,128]{3,0,2,1:T(8,128)(2,1)S(1)}, u32[]{:S(2)}, u32[]{:S(2)}) collective-permute-start(bf16[64,1,8,128]{3,0,2,1:T(8,128)(2,1)S(1)} %get-tuple-element.508), channel_id=1, source_target_pairs={{113,0},{0,1},{1,16},{16,17},{17,32},{32,33},{33,48},{48,49},{49,6... | collective-permute-start | bytes 393224 | tf_op jit(solution)/shard_map/while/body/eval_jaxpr/ppermute | solution.py:18
  169.0 3.6 collective-permute-start.3
  169.1 4.6 collective-permute-start.4
  175.1 6.6 %collective-permute-start.1 = (bf16[64,1,8,128]{3,0,2,1:T(8,128)(2,1)S(1)}, bf16[64,1,8,128]{3,0,2,1:T(8,128)(2,1)S(1)}, u32[]{:S(2)}, u32[]{:S(2)}) collective-permute-start(bf16[64,1,8,128]{3,0,2,1:T(8,128)(2,1)S(1)} %get-tuple-element.508), channel_id=1, source_target_pairs={{113,0},{0,1},{1,16},{16,17},{17,32},{32,33},{33,48},{48,49},{49,6... | collective-permute-start | bytes 393224 | tf_op jit(solution)/shard_map/while/body/eval_jaxpr/ppermute | solution.py:18
  179.8 3.6 collective-permute-start.3
  179.9 4.6 collective-permute-start.4
  185.9 5.4 %collective-permute-start.6 = (bf16[64,1,8]{0,2,1:T(8,128)(2,1)S(1)}, bf16[64,1,8]{0,2,1:T(8,128)(2,1)S(1)}, u32[]{:S(2)}, u32[]{:S(2)}) collective-permute-start(bf16[64,1,8]{0,2,1:T(8,128)(2,1)S(1)} %convert_element_type.51), channel_id=1, source_target_pairs={{113,0},{0,1},{1,16},{16,17},{17,32},{32,33},{33,48},{48,49},{49,6... | collective-permute-start | bytes 3080 | tf_op jit(solution)/shard_map/ppermute | solution.py:18
  193.4 278.7 %reduce-scatter.2.cloned.1.call-start = ((), (), s32[]{:S(2)}) async-start(), calls=%async_computation.2 | async-start | bytes 1179648 | tf_op jit(solution)/shard_map/reduce_scatter | solution.py:141
  242.4 3.6 collective-permute-start
  253.1 7.7 %collective-permute-start = (bf16[512,1,2,128]{3,0,2,1:T(8,128)(2,1)}, bf16[512,1,2,128]{3,0,2,1:T(8,128)(2,1)S(1)}, u32[]{:S(2)}, u32[]{:S(2)}) collective-permute-start(bf16[512,1,2,128]{3,0,2,1:T(8,128)(2,1)} %get-tuple-element.479), channel_id=1, source_target_pairs={{0,1},{1,16},{16,17},{17,32},{32,33},{33,48},{48,49},{49,64},{64,6... | collective-permute-start | bytes 786440 | tf_op jit(solution)/shard_map/while/body/eval_jaxpr/ppermute | solution.py:12
  267.8 8.3 %collective-permute-start = (bf16[512,1,2,128]{3,0,2,1:T(8,128)(2,1)}, bf16[512,1,2,128]{3,0,2,1:T(8,128)(2,1)S(1)}, u32[]{:S(2)}, u32[]{:S(2)}) collective-permute-start(bf16[512,1,2,128]{3,0,2,1:T(8,128)(2,1)} %get-tuple-element.479), channel_id=1, source_target_pairs={{0,1},{1,16},{16,17},{17,32},{32,33},{33,48},{48,49},{49,64},{64,6... | collective-permute-start | bytes 786440 | tf_op jit(solution)/shard_map/while/body/eval_jaxpr/ppermute | solution.py:12
  283.2 8.4 %collective-permute-start = (bf16[512,1,2,128]{3,0,2,1:T(8,128)(2,1)}, bf16[512,1,2,128]{3,0,2,1:T(8,128)(2,1)S(1)}, u32[]{:S(2)}, u32[]{:S(2)}) collective-permute-start(bf16[512,1,2,128]{3,0,2,1:T(8,128)(2,1)} %get-tuple-element.479), channel_id=1, source_target_pairs={{0,1},{1,16},{16,17},{17,32},{32,33},{33,48},{48,49},{49,64},{64,6... | collective-permute-start | bytes 786440 | tf_op jit(solution)/shard_map/while/body/eval_jaxpr/ppermute | solution.py:12
  298.7 9.3 %collective-permute-start = (bf16[512,1,2,128]{3,0,2,1:T(8,128)(2,1)}, bf16[512,1,2,128]{3,0,2,1:T(8,128)(2,1)S(1)}, u32[]{:S(2)}, u32[]{:S(2)}) collective-permute-start(bf16[512,1,2,128]{3,0,2,1:T(8,128)(2,1)} %get-tuple-element.479), channel_id=1, source_target_pairs={{0,1},{1,16},{16,17},{17,32},{32,33},{33,48},{48,49},{49,64},{64,6... | collective-permute-start | bytes 786440 | tf_op jit(solution)/shard_map/while/body/eval_jaxpr/ppermute | solution.py:12
  315.1 7.9 %collective-permute-start = (bf16[512,1,2,128]{3,0,2,1:T(8,128)(2,1)}, bf16[512,1,2,128]{3,0,2,1:T(8,128)(2,1)S(1)}, u32[]{:S(2)}, u32[]{:S(2)}) collective-permute-start(bf16[512,1,2,128]{3,0,2,1:T(8,128)(2,1)} %get-tuple-element.479), channel_id=1, source_target_pairs={{0,1},{1,16},{16,17},{17,32},{32,33},{33,48},{48,49},{49,64},{64,6... | collective-permute-start | bytes 786440 | tf_op jit(solution)/shard_map/while/body/eval_jaxpr/ppermute | solution.py:12
  330.0 7.9 %collective-permute-start = (bf16[512,1,2,128]{3,0,2,1:T(8,128)(2,1)}, bf16[512,1,2,128]{3,0,2,1:T(8,128)(2,1)S(1)}, u32[]{:S(2)}, u32[]{:S(2)}) collective-permute-start(bf16[512,1,2,128]{3,0,2,1:T(8,128)(2,1)} %get-tuple-element.479), channel_id=1, source_target_pairs={{0,1},{1,16},{16,17},{17,32},{32,33},{33,48},{48,49},{49,64},{64,6... | collective-permute-start | bytes 786440 | tf_op jit(solution)/shard_map/while/body/eval_jaxpr/ppermute | solution.py:12
  345.0 7.9 %collective-permute-start = (bf16[512,1,2,128]{3,0,2,1:T(8,128)(2,1)}, bf16[512,1,2,128]{3,0,2,1:T(8,128)(2,1)S(1)}, u32[]{:S(2)}, u32[]{:S(2)}) collective-permute-start(bf16[512,1,2,128]{3,0,2,1:T(8,128)(2,1)} %get-tuple-element.479), channel_id=1, source_target_pairs={{0,1},{1,16},{16,17},{17,32},{32,33},{33,48},{48,49},{49,64},{64,6... | collective-permute-start | bytes 786440 | tf_op jit(solution)/shard_map/while/body/eval_jaxpr/ppermute | solution.py:12
  359.9 7.9 %collective-permute-start = (bf16[512,1,2,128]{3,0,2,1:T(8,128)(2,1)}, bf16[512,1,2,128]{3,0,2,1:T(8,128)(2,1)S(1)}, u32[]{:S(2)}, u32[]{:S(2)}) collective-permute-start(bf16[512,1,2,128]{3,0,2,1:T(8,128)(2,1)} %get-tuple-element.479), channel_id=1, source_target_pairs={{0,1},{1,16},{16,17},{17,32},{32,33},{33,48},{48,49},{49,64},{64,6... | collective-permute-start | bytes 786440 | tf_op jit(solution)/shard_map/while/body/eval_jaxpr/ppermute | solution.py:12
  374.9 7.9 %collective-permute-start = (bf16[512,1,2,128]{3,0,2,1:T(8,128)(2,1)}, bf16[512,1,2,128]{3,0,2,1:T(8,128)(2,1)S(1)}, u32[]{:S(2)}, u32[]{:S(2)}) collective-permute-start(bf16[512,1,2,128]{3,0,2,1:T(8,128)(2,1)} %get-tuple-element.479), channel_id=1, source_target_pairs={{0,1},{1,16},{16,17},{17,32},{32,33},{33,48},{48,49},{49,64},{64,6... | collective-permute-start | bytes 786440 | tf_op jit(solution)/shard_map/while/body/eval_jaxpr/ppermute | solution.py:12
  389.9 8.0 %collective-permute-start = (bf16[512,1,2,128]{3,0,2,1:T(8,128)(2,1)}, bf16[512,1,2,128]{3,0,2,1:T(8,128)(2,1)S(1)}, u32[]{:S(2)}, u32[]{:S(2)}) collective-permute-start(bf16[512,1,2,128]{3,0,2,1:T(8,128)(2,1)} %get-tuple-element.479), channel_id=1, source_target_pairs={{0,1},{1,16},{16,17},{17,32},{32,33},{33,48},{48,49},{49,64},{64,6... | collective-permute-start | bytes 786440 | tf_op jit(solution)/shard_map/while/body/eval_jaxpr/ppermute | solution.py:12
  405.0 8.8 %collective-permute-start = (bf16[512,1,2,128]{3,0,2,1:T(8,128)(2,1)}, bf16[512,1,2,128]{3,0,2,1:T(8,128)(2,1)S(1)}, u32[]{:S(2)}, u32[]{:S(2)}) collective-permute-start(bf16[512,1,2,128]{3,0,2,1:T(8,128)(2,1)} %get-tuple-element.479), channel_id=1, source_target_pairs={{0,1},{1,16},{16,17},{17,32},{32,33},{33,48},{48,49},{49,64},{64,6... | collective-permute-start | bytes 786440 | tf_op jit(solution)/shard_map/while/body/eval_jaxpr/ppermute | solution.py:12
  420.8 8.8 %collective-permute-start = (bf16[512,1,2,128]{3,0,2,1:T(8,128)(2,1)}, bf16[512,1,2,128]{3,0,2,1:T(8,128)(2,1)S(1)}, u32[]{:S(2)}, u32[]{:S(2)}) collective-permute-start(bf16[512,1,2,128]{3,0,2,1:T(8,128)(2,1)} %get-tuple-element.479), channel_id=1, source_target_pairs={{0,1},{1,16},{16,17},{17,32},{32,33},{33,48},{48,49},{49,64},{64,6... | collective-permute-start | bytes 786440 | tf_op jit(solution)/shard_map/while/body/eval_jaxpr/ppermute | solution.py:12
  436.7 8.8 %collective-permute-start = (bf16[512,1,2,128]{3,0,2,1:T(8,128)(2,1)}, bf16[512,1,2,128]{3,0,2,1:T(8,128)(2,1)S(1)}, u32[]{:S(2)}, u32[]{:S(2)}) collective-permute-start(bf16[512,1,2,128]{3,0,2,1:T(8,128)(2,1)} %get-tuple-element.479), channel_id=1, source_target_pairs={{0,1},{1,16},{16,17},{17,32},{32,33},{33,48},{48,49},{49,64},{64,6... | collective-permute-start | bytes 786440 | tf_op jit(solution)/shard_map/while/body/eval_jaxpr/ppermute | solution.py:12
  452.6 8.8 %collective-permute-start = (bf16[512,1,2,128]{3,0,2,1:T(8,128)(2,1)}, bf16[512,1,2,128]{3,0,2,1:T(8,128)(2,1)S(1)}, u32[]{:S(2)}, u32[]{:S(2)}) collective-permute-start(bf16[512,1,2,128]{3,0,2,1:T(8,128)(2,1)} %get-tuple-element.479), channel_id=1, source_target_pairs={{0,1},{1,16},{16,17},{17,32},{32,33},{33,48},{48,49},{49,64},{64,6... | collective-permute-start | bytes 786440 | tf_op jit(solution)/shard_map/while/body/eval_jaxpr/ppermute | solution.py:12
  (18 other events, 443.0 us)
Sparse Core Ops, SparseCore 0:
  193.6 35.3 all-gather.1
  233.1 70.6 reduce-scatter.1
where the time goes:
time: 481 us; the launch traced here: 479 us
  waiting for transfers between devices  172 us (36%)
  matrix products  134 us (28%)
  starting transfers between devices  94.1 us (20%)
  other arithmetic  36 us (7%)
  local copies, waits for them, and re-layouts  26.8 us (6%)
  between operations  14.2 us (3%)
    ppermute x15, waiting for transfers between devices, passed_along(): return lax.ppermute(value, axis, pairs)  100 us
    ppermute x62, starting transfers between devices, shifted(): return lax.ppermute(block, axis, route)  74.6 us
    dot_general x33, matrix products, absorb(): jnp.einsum(out_form, weights.astype(jnp.bfloat16), values, preferred_elem...  65.6 us
    dot_general x32, matrix products, with_keys(): jnp.einsum('rhgd,thd->rhgt', queries, keys, preferred_element_type=jnp.fl...  63.4 us
    ppermute x62, waiting for transfers between devices, shifted(): return lax.ppermute(block, axis, route)  43 us
    all_gather x1, waiting for transfers between devices, on_device(): lax.all_gather(attended, ('ctx', 'rep'), axis=0, tiled=True)  28.4 us
    reduce_sum x17, other arithmetic, absorb(): running_sum = running_sum * factor + jnp.sum(weights, axis=-1)  25.5 us
    ppermute x15, starting transfers between devices, passed_along(): return lax.ppermute(value, axis, pairs)  19.2 us
  transfers between devices with their start and end apart: 79, of which 48 were waited for; matrix products, arithmetic and copies ran while one was open for 32% of the time, Pallas kernels for 0%

commit v1 on v0

v1 whole, which is shorter than its diff:
```python
import functools

import jax
import jax.numpy as jnp
from jax import lax
from jax.experimental import pallas as pl
from jax.experimental.pallas import tpu as pltpu
from jax.sharding import PartitionSpec as P

F32, BF16 = jnp.float32, jnp.bfloat16
MESH = pl.DeviceIdType.MESH
LOW_FILL = -1e30
WIDTH = 128
SCALE = WIDTH**-0.5 * 1.4426950408889634
BLOCK = 512
CHUNK = 512
CHUNKS = 8
GUESTS = 4
SLOTS = 1 + CHUNKS + GUESTS
NT = (((1,), (1,)), ((), ()))


def wide(column, width):
    return jnp.concatenate([column] * (width // WIDTH), axis=1)


def kernel(
    q_hbm, kv_hbm, dq_hbm, tail_hbm, len_ref, w_hbm,
    out_hbm, dec_ref,
    kvint, kbuf, vbuf, qbuf, tailbuf, wbuf, m_ref, l_ref, acc_ref,
    obuf, fbuf, att, part, landed,
    in_sem, q_sem, send_sem, kv_sem, att_sem, guest_sem, back_sem, rs_sem, out_sem,
):
    ctx, head, rep = lax.axis_index("ctx"), lax.axis_index("head"), lax.axis_index("rep")
    z, x = ctx // 2, ctx % 2
    me = ctx * 2 + rep
    mate = 15 - me
    late = me >= 8
    guests = jnp.where(late, 0, mate // 2 - 3)
    given = jnp.where(late, me // 2 - 3, 0)
    own_base = 1 + guests
    own_count = CHUNKS - given

    def place(dz, flip):
        return ((z + dz) % 4) * 2 + (1 - x if flip else x)

    chips = [ctx, place(0, True), place(1, False), place(3, False),
             place(1, True), place(3, True), place(2, False), place(2, True)]
    OWN, XP, ZP, ZM, ZPX, ZMX, ZZ, ZZX = range(8)

    sibling = {"ctx": ctx, "rep": 1 - rep}
    over_x = {"ctx": chips[XP], "rep": rep}
    over_zp = {"ctx": chips[ZP], "rep": rep}
    over_zm = {"ctx": chips[ZM], "rep": rep}
    to_mate = {"ctx": mate // 2, "rep": mate % 2}

    def load(src, dst, sem):
        copy = pltpu.make_async_copy(src, dst, sem)
        copy.start()
        return copy

    kv_in = load(kv_hbm, kvint, in_sem.at[0])
    dq_in = load(dq_hbm, qbuf.at[pl.ds(0, CHUNK)], in_sem.at[1])

    def own_q(k):
        return pltpu.make_async_copy(
            q_hbm.at[pl.ds(pl.multiple_of((given + k) * CHUNK, CHUNK), CHUNK)],
            qbuf.at[pl.ds(pl.multiple_of((own_base + k) * CHUNK, CHUNK), CHUNK)],
            q_sem.at[k],
        )

    for k in range(CHUNKS):
        @pl.when(k < own_count)
        def _(k=k):
            own_q(k).start()

    tail_in = load(tail_hbm, tailbuf, in_sem.at[2])
    w_in = load(w_hbm, wbuf, in_sem.at[3])

    barrier = pltpu.get_barrier_semaphore()
    for device in (sibling, over_x, over_zp, over_zm, to_mate):
        pl.semaphore_signal(barrier, inc=1, device_id=device, device_id_type=MESH)
    for away in range(1, 8):
        pl.semaphore_signal(
            barrier, inc=1, device_id={"head": (head + away) % 8}, device_id_type=MESH
        )

    rows = lax.broadcasted_iota(jnp.int32, (256, 256), 0)
    cols = lax.broadcasted_iota(jnp.int32, (256, 256), 1)
    wanted = jnp.where(rows < 128, rows * 2, (rows - 128) * 2 + 1)
    pick = jnp.where(cols == wanted, 1.0, 0.0).astype(BF16)
    kv_in.wait()
    for t in range(4):
        apart = jnp.dot(pick, kvint[t * 256:(t + 1) * 256, :], preferred_element_type=F32)
        apart = apart.astype(BF16)
        here = pl.ds(pl.multiple_of(me * BLOCK + t * 128, 128), 128)
        kbuf[here, :] = apart[:128]
        vbuf[here, :] = apart[128:]

    pl.semaphore_wait(barrier, 12)

    sends = []

    def block_of(which, s, kind, piece):
        b = chips[s] * 2 + (rep if kind == 0 else 1 - rep)
        if which == "kv":
            ref = kbuf if piece == 0 else vbuf
            return ref.at[pl.ds(pl.multiple_of(b * BLOCK, BLOCK), BLOCK)]
        return att.at[pl.ds(pl.multiple_of(b * 64 + piece * 32, 32), 32)]

    def sem_of(which):
        return kv_sem if which == "kv" else att_sem

    def send(which, s, piece, device, s_there, kind_there):
        copy = pltpu.make_async_remote_copy(
            src_ref=block_of(which, s, 0, piece),
            dst_ref=block_of(which, s, 0, piece),
            send_sem=send_sem.at[len(sends)],
            recv_sem=sem_of(which).at[s_there, kind_there, piece],
            device_id=device,
            device_id_type=MESH,
        )
        copy.start()
        sends.append(copy)

    def arrived(which, s, kind, pieces=(0, 1)):
        for piece in pieces:
            ref = block_of(which, s, kind, piece)
            pltpu.make_async_remote_copy(
                src_ref=ref, dst_ref=ref, send_sem=send_sem.at[0],
                recv_sem=sem_of(which).at[s, kind, piece],
                device_id=sibling, device_id_type=MESH,
            ).wait_recv()

    def both(which, s, device, s_there, kind_there):
        for piece in (0, 1):
            send(which, s, piece, device, s_there, kind_there)

    def gather_start(which):
        both(which, OWN, over_zp, ZM, 0)
        both(which, OWN, over_zm, ZP, 0)
        both(which, OWN, over_x, XP, 0)
        both(which, OWN, sibling, OWN, 1)

    def gather_first(which):
        arrived(which, XP, 0)
        both(which, XP, over_zp, ZMX, 0)
        both(which, XP, over_zm, ZPX, 0)
        both(which, XP, sibling, XP, 1)
        arrived(which, ZM, 0)
        send(which, ZM, 0, over_zp, ZZ, 0)
        both(which, ZM, sibling, ZM, 1)
        arrived(which, ZP, 0)
        send(which, ZP, 1, over_zm, ZZ, 0)
        both(which, ZP, sibling, ZP, 1)

    def gather_second(which):
        arrived(which, ZMX, 0)
        send(which, ZMX, 0, over_zp, ZZX, 0)
        both(which, ZMX, sibling, ZMX, 1)
        arrived(which, ZPX, 0)
        send(which, ZPX, 1, over_zm, ZZX, 0)
        both(which, ZPX, sibling, ZPX, 1)

    def gather_third(which):
        arrived(which, ZZ, 0)
        both(which, ZZ, sibling, ZZ, 1)
        arrived(which, ZZX, 0)
        both(which, ZZX, sibling, ZZX, 1)

    gather_start("kv")

    def guest_q(k):
        return pltpu.make_async_remote_copy(
            src_ref=q_hbm.at[pl.ds(k * CHUNK, CHUNK)],
            dst_ref=qbuf.at[pl.ds((1 + k) * CHUNK, CHUNK)],
            send_sem=guest_sem.at[0, k], recv_sem=guest_sem.at[1, k],
            device_id=to_mate, device_id_type=MESH,
        )

    for k in range(GUESTS):
        @pl.when(k < given)
        def _(k=k):
            guest_q(k).start()

    def rows_of(slot):
        return pl.ds(pl.multiple_of(slot * CHUNK, CHUNK), CHUNK)

    def absorb(slots, first_key, keys, first_place=None):
        key_rows = pl.ds(pl.multiple_of(first_key, keys), keys)
        where = [rows_of(slot) for slot in slots]
        m_old = [m_ref[r, :] for r in where]
        l_old = [l_ref[r, :] for r in where]
        a_old = [acc_ref[r, :] for r in where]
        scores = [
            lax.dot_general(qbuf[r, :], kbuf[key_rows, :], NT, preferred_element_type=F32)
            for r in where
        ]
        result = []
        for i in range(len(slots)):
            s = scores[i]
            if first_place is not None:
                row = lax.broadcasted_iota(jnp.int32, s.shape, 0) // 8 + first_place[i]
                s = jnp.where(lax.broadcasted_iota(jnp.int32, s.shape, 1) <= row, s, LOW_FILL)
            m_new = jnp.maximum(m_old[i], jnp.max(s, axis=1, keepdims=True))
            p = jnp.exp2((s - wide(m_new, keys)) * SCALE)
            factor = jnp.exp2((m_old[i] - m_new) * SCALE)
            total = p[:, :WIDTH]
            for j in range(1, keys // WIDTH):
                total = total + p[:, j * WIDTH:(j + 1) * WIDTH]
            mixed = jnp.dot(p.astype(BF16), vbuf[key_rows, :], preferred_element_type=F32)
            result.append((m_new, l_old[i] * factor + total, a_old[i] * factor + mixed))
        for i, r in enumerate(where):
            m_ref[r, :], l_ref[r, :], acc_ref[r, :] = result[i]

    def sweep(first, count, first_key, keys, place=None):
        def at(slot):
            return None if place is None else [(s - first + place) * 64 for s in slot]

        def pair(t, _):
            slots = [first + 2 * t, first + 2 * t + 1]
            absorb(slots, first_key, keys, at(slots))
            return 0

        lax.fori_loop(0, count // 2, pair, 0)

        @pl.when(count % 2 == 1)
        def _():
            slots = [first + count - 1]
            absorb(slots, first_key, keys, at(slots))

    def others(chip):
        mine = jnp.where(chip < me // 2, own_count, 0)
        theirs = jnp.where(jnp.logical_and(jnp.logical_not(late), chip < mate // 2), guests, 0)
        return mine + theirs

    def both_blocks(chip):
        sweep(1, others(chip), chip * 2 * BLOCK, 2 * BLOCK)

    def decode_step(chip):
        absorb([0], chip * 2 * BLOCK, 2 * BLOCK)

    m_ref[CHUNK:, :] = jnp.full((CHUNK * (SLOTS - 1), WIDTH), LOW_FILL, F32)
    l_ref[CHUNK:, :] = jnp.zeros((CHUNK * (SLOTS - 1), WIDTH), F32)
    acc_ref[CHUNK:, :] = jnp.zeros((CHUNK * (SLOTS - 1), WIDTH), F32)

    for k in range(CHUNKS):
        @pl.when(k < own_count)
        def _(k=k):
            own_q(k).wait()

    sweep(own_base, own_count, me * BLOCK, BLOCK, given)
    gather_first("kv")

    dq_in.wait()
    tail_in.wait()

    def tail_step(t, _):
        first = t * 8
        scores, kv = [], []
        col = lax.broadcasted_iota(jnp.int32, (8, 256), 1)
        for u in range(8):
            r = first + u
            kv.append(pl.ds(pl.multiple_of(r * 256, 256), 256))
            q16 = qbuf[pl.ds(pl.multiple_of((first + u // 2 * 2) * 8, 16), 16), :]
            s = lax.dot_general(q16, tailbuf[kv[u], :], NT, preferred_element_type=F32)
            s = s[u % 2 * 8:u % 2 * 8 + 8]
            seen = jnp.logical_and(col % 2 == 0, col < 2 * len_ref[r])
            scores.append(jnp.where(seen, s, LOW_FILL))
        s = jnp.concatenate(scores, axis=0)
        m_new = jnp.broadcast_to(jnp.max(s, axis=1, keepdims=True), (64, WIDTH))
        p = jnp.exp2((s - wide(m_new, 256)) * SCALE)
        here = pl.ds(pl.multiple_of(t * 64, 64), 64)
        m_ref[here, :] = m_new
        l_ref[here, :] = p[:, :WIDTH] + p[:, WIDTH:]
        p = pltpu.roll(p, 1, 1).astype(BF16)
        out = []
        for u in range(8):
            p16 = p[u // 2 * 16:u // 2 * 16 + 16]
            o = jnp.dot(p16, tailbuf[kv[u], :], preferred_element_type=F32)
            out.append(o[u % 2 * 8:u % 2 * 8 + 8])
        acc_ref[here, :] = jnp.concatenate(out, axis=0)
        return 0

    lax.fori_loop(0, 8, tail_step, 0)

    arrived("kv", OWN, 1)
    decode_step(ctx)

    @pl.when(rep == 1)
    def _():
        sweep(own_base, own_count, (me - 1) * BLOCK, BLOCK)

    for k in range(GUESTS):
        @pl.when(k < guests)
        def _(k=k):
            guest_q(k).wait_recv()

    both_blocks(ctx)
    arrived("kv", XP, 1)
    decode_step(chips[XP])
    both_blocks(chips[XP])
    gather_second("kv")
    arrived("kv", ZM, 1)
    decode_step(chips[ZM])
    arrived("kv", ZP, 1)
    decode_step(chips[ZP])
    both_blocks(chips[ZM])
    gather_third("kv")
    for s in (ZMX, ZPX, ZZ, ZZX):
        arrived("kv", s, 1)
        decode_step(chips[s])

    total = jnp.sum(l_ref[:CHUNK, :], axis=1, keepdims=True)
    fbuf[...] = acc_ref[:CHUNK, :] / total
    mine = pl.ds(pl.multiple_of(me * 64, 64), 64)
    for h in range(8):
        att[mine, h * WIDTH:(h + 1) * WIDTH] = fbuf[pl.ds(h, 64, stride=8), :].astype(BF16)
    gather_start("att")

    both_blocks(chips[ZP])
    gather_first("att")
    both_blocks(chips[ZMX])
    gather_second("att")
    both_blocks(chips[ZPX])
    gather_third("att")

    w_in.wait()

    def rs_copy(chip, sem):
        return pltpu.make_async_remote_copy(
            src_ref=part.at[pl.ds(pl.multiple_of(chip * 128, 128), 128)],
            dst_ref=landed.at[pl.ds(pl.multiple_of(head * 128, 128), 128)],
            send_sem=rs_sem.at[0, sem], recv_sem=rs_sem.at[1, head],
            device_id={"head": chip}, device_id_type=MESH,
        )

    arrived("att", OWN, 1)
    for s in range(1, 8):
        arrived("att", s, 1)

    def project(k, _):
        chip = (head + k) % 8
        rows_here = pl.ds(pl.multiple_of(chip * 128, 128), 128)
        part[rows_here, :] = jnp.dot(
            att[rows_here, :], wbuf[...], preferred_element_type=F32
        ).astype(BF16)

        @pl.when(k > 0)
        def _():
            rs_copy(chip, k).start()

        return 0

    lax.fori_loop(0, 8, project, 0)

    both_blocks(chips[ZZ])
    both_blocks(chips[ZZX])

    @pl.when(guests > 0)
    def _():
        sweep(1, guests, mate * BLOCK, BLOCK, 0)

        @pl.when(mate % 2 == 1)
        def _():
            sweep(1, guests, (mate - 1) * BLOCK, BLOCK)

    def finish(slot):
        r = rows_of(slot)
        obuf[r, :] = (
            acc_ref[r, :] / jnp.sum(l_ref[r, :], axis=1, keepdims=True)
        ).astype(BF16)

    def give_back(k):
        return pltpu.make_async_remote_copy(
            src_ref=obuf.at[pl.ds((1 + k) * CHUNK, CHUNK)],
            dst_ref=out_hbm.at[pl.ds(k * CHUNK, CHUNK)],
            send_sem=back_sem.at[0, k], recv_sem=back_sem.at[1, k],
            device_id=to_mate, device_id_type=MESH,
        )

    for k in range(GUESTS):
        @pl.when(k < guests)
        def _(k=k):
            finish(1 + k)
            give_back(k).start()

    def own_out(k):
        return pltpu.make_async_copy(
            obuf.at[pl.ds(pl.multiple_of((own_base + k) * CHUNK, CHUNK), CHUNK)],
            out_hbm.at[pl.ds(pl.multiple_of((given + k) * CHUNK, CHUNK), CHUNK)],
            out_sem.at[k],
        )

    for k in range(CHUNKS):
        @pl.when(k < own_count)
        def _(k=k):
            finish(own_base + k)
            own_out(k).start()

    mine = pl.ds(pl.multiple_of(head * 128, 128), 128)
    total = part[mine, :].astype(F32)
    for away in range(1, 8):
        other = (head + away) % 8
        there = landed.at[pl.ds(pl.multiple_of(other * 128, 128), 128)]
        pltpu.make_async_remote_copy(
            src_ref=there, dst_ref=there, send_sem=rs_sem.at[0, 0],
            recv_sem=rs_sem.at[1, other], device_id={"head": other}, device_id_type=MESH,
        ).wait_recv()
        total = total + landed[pl.ds(pl.multiple_of(other * 128, 128), 128), :].astype(F32)
    dec_ref[...] = total.astype(BF16)

    for copy in sends:
        copy.wait_send()
    for k in range(1, 8):
        rs_copy((head + k) % 8, k).wait_send()
    for k in range(GUESTS):
        @pl.when(k < given)
        def _(k=k):
            guest_q(k).wait_send()
            give_back(k).wait_recv()

        @pl.when(k < guests)
        def _(k=k):
            give_back(k).wait_send()
    for k in range(CHUNKS):
        @pl.when(k < own_count)
        def _(k=k):
            own_out(k).wait()


def on_device(prefix_query, prefix_kv, decode_query, tail_key_value, tail_len, out_weight):
    any_space = pl.BlockSpec(memory_space=pl.ANY)
    prefix_out, decoded = pl.pallas_call(
        kernel,
        out_shape=(
            jax.ShapeDtypeStruct((CHUNKS * CHUNK, WIDTH), BF16),
            jax.ShapeDtypeStruct((128, 512), BF16),
        ),
        in_specs=[any_space] * 4 + [pl.BlockSpec(memory_space=pltpu.SMEM), any_space],
        out_specs=(any_space, pl.BlockSpec(memory_space=pltpu.VMEM)),
        scratch_shapes=[
            pltpu.VMEM((2 * BLOCK, WIDTH), BF16),
            pltpu.VMEM((16 * BLOCK, WIDTH), BF16),
            pltpu.VMEM((16 * BLOCK, WIDTH), BF16),
            pltpu.VMEM((SLOTS * CHUNK, WIDTH), BF16),
            pltpu.VMEM((64 * 256, WIDTH), BF16),
            pltpu.VMEM((1024, 512), BF16),
            pltpu.VMEM((SLOTS * CHUNK, WIDTH), F32),
            pltpu.VMEM((SLOTS * CHUNK, WIDTH), F32),
            pltpu.VMEM((SLOTS * CHUNK, WIDTH), F32),
            pltpu.VMEM((SLOTS * CHUNK, WIDTH), BF16),
            pltpu.VMEM((CHUNK, WIDTH), F32),
            pltpu.VMEM((1024, 1024), BF16),
            pltpu.VMEM((1024, 512), BF16),
            pltpu.VMEM((1024, 512), BF16),
            pltpu.SemaphoreType.DMA((4,)),
            pltpu.SemaphoreType.DMA((CHUNKS,)),
            pltpu.SemaphoreType.DMA((64,)),
            pltpu.SemaphoreType.DMA((8, 2, 2)),
            pltpu.SemaphoreType.DMA((8, 2, 2)),
            pltpu.SemaphoreType.DMA((2, GUESTS)),
            pltpu.SemaphoreType.DMA((2, GUESTS)),
            pltpu.SemaphoreType.DMA((2, 8)),
            pltpu.SemaphoreType.DMA((CHUNKS,)),
        ],
        compiler_params=pltpu.CompilerParams(
            collective_id=0, has_side_effects=True, vmem_limit_bytes=56 << 20
        ),
        name="layer_attention",
    )(
        prefix_query.reshape(CHUNKS * CHUNK, WIDTH),
        prefix_kv.reshape(2 * BLOCK, WIDTH),
        decode_query.reshape(CHUNK, WIDTH),
        tail_key_value.reshape(64 * 256, WIDTH),
        tail_len,
        out_weight,
    )
    return prefix_out.reshape(prefix_query.shape), decoded


def solution(mesh):
    return jax.shard_map(
        on_device,
        mesh=mesh,
        in_specs=(
            P(("ctx", "rep"), "head", None),
            P(("ctx", "rep"), "head", None, None),
            P(("ctx", "rep"), "head", None),
            P(("ctx", "rep"), None, "head", None, None),
            P(("ctx", "rep")),
            P("head", ("ctx", "rep")),
        ),
        out_specs=(P(("ctx", "rep"), "head", None), P("head", ("ctx", "rep"))),
        check_vma=False,
    )
```

time: 481 us -> 95.9 us (0.20)
  waiting for transfers between devices: 172 us -> 0 us
  matrix products: 134 us -> 0 us
  starting transfers between devices: 94.1 us -> 0 us
  Pallas kernels: 0 us -> 90.1 us
  other arithmetic: 36 us -> 0 us
  local copies, waits for them, and re-layouts: 26.8 us -> 3.83 us
  between operations: 14.2 us -> 0.64 us
    ppermute x77 -> x0, waiting for transfers between devices: 143 us -> none  [the longest x15 100 us: passed_along(): return lax.ppermute(value, axis, pairs)]
    dot_general x67 -> x0, matrix products: 134 us -> none  [the longest x33 65.6 us: absorb(): jnp.einsum(out_form, weights.astype(jnp.bfloat16), values, preferred_elem...]
    ppermute x77 -> x0, starting transfers between devices: 93.8 us -> none  [the longest x62 74.6 us: shifted(): return lax.ppermute(block, axis, route)]
    pallas_call x0 -> x1, Pallas kernels: none -> 90.1 us  [on_device(): pl.pallas_call(kernel, out_shape=(jax.ShapeDtypeStruct((CHUNKS * CHUNK, W...]
    all_gather x1 -> x0, waiting for transfers between devices: 28.4 us -> none  [on_device(): lax.all_gather(attended, ('ctx', 'rep'), axis=0, tiled=True)]
    reduce_sum x17 -> x0, other arithmetic: 25.5 us -> none  [absorb(): running_sum = running_sum * factor + jnp.sum(weights, axis=-1)]
    while x31 -> x0, local copies, waits for them, and re-layouts: 12.3 us -> none
    slice x1 -> x0, local copies, waits for them, and re-layouts: 9.76 us -> none  [on_device(): tail_key_value[:, :, :, 1, :]]
  transfers between devices with their start and end apart: 79 -> 0, of which waited for: 48 -> 0; matrix products, arithmetic and copies ran while one was open for 32% -> 0% of each run, Pallas kernels for 0% -> 0%
where the time goes in v1:
time: 95.9 us; the launch traced here: 94.6 us
  Pallas kernels  90.1 us (94%)
  local copies, waits for them, and re-layouts  3.83 us (4%)
    pallas_call x1, Pallas kernels, on_device(): pl.pallas_call(kernel, out_shape=(jax.ShapeDtypeStruct((CHUNKS * CHUNK, W...  90.1 us
    unnamed x2, local copies, waits for them, and re-layouts  3.83 us

profile of v1, /device:TPU:99, one launch (start us, length us, event | category | flops | bytes accessed | tf_op | source)
XLA Modules:
  0.0 94.6 jit_solution(12834777994114801561)
XLA Ops:
  0.6 90.1 %layer_attention.1 = (bf16[4096,128]{1,0:T(8,128)(2,1)}, bf16[128,512]{1,0:T(8,128)(2,1)}) custom-call(bf16[4096,128]{1,0:T(8,128)(2,1)} %bitcast.7, bf16[1024,128]{1,0:T(8,128)(2,1)} %bitcast.8, bf16[512,128]{1,0:T(8,128)(2,1)} %bitcast.9, bf16[16384,128]{1,0:T(8,128)(2,1)} %bitcast.5, s32[64]{0:T(128)} %len_ref.1, bf16[1024,512]{1,0:T(8,128)(2,1)} %w_hbm.1), custom_call_target="tpu_custom_call" | custom-call | tf_op jit(solution)/shard_map/layer_attention/pallas_call | solution.py:434
  90.8 2.3 %copy.10 = bf16[512,8,128]{2,1,0:T(8,128)(2,1)} copy(bf16[512,8,128]{2,1,0:T(8,128)(2,1)} %bitcast.6) | data formatting | bytes 2097152
  93.0 1.6 %copy.11 = bf16[128,512]{1,0:T(8,128)(2,1)} copy(bf16[128,512]{1,0:T(8,128)(2,1)} %get-tuple-element.9) | data formatting | bytes 262144

commit v2 on v1

v2 whole, which is shorter than its diff:
```python
import functools

import jax
import jax.numpy as jnp
from jax import lax
from jax.experimental import pallas as pl
from jax.experimental.pallas import tpu as pltpu
from jax.sharding import PartitionSpec as P

F32, BF16 = jnp.float32, jnp.bfloat16
MESH = pl.DeviceIdType.MESH
LOW_FILL = -1e30
WIDTH = 128
SCALE = WIDTH**-0.5 * 1.4426950408889634
BLOCK = 512
CHUNK = 512
CHUNKS = 8
GUESTS = 4
GUEST_BASE = 1 + CHUNKS
SLOTS = 1 + CHUNKS + GUESTS + 1
NT = (((1,), (1,)), ((), ()))
EARLY = 1
ROLLS = 16
ITEMS = (3, 4)


def wide(column, width):
    return jnp.concatenate([column] * (width // WIDTH), axis=1)


def kernel(
    q_hbm, kv_hbm, dq_hbm, tail_hbm, len_ref, w_hbm,
    out_hbm, landed,
    kvint, kbuf, vbuf, qbuf, tailbuf, wbuf, m_ref, l_ref, acc_ref,
    obuf, fbuf, ahead, att, part,
    in_sem, q_sem, send_sem, kv_sem, att_sem, guest_sem, back_sem, rs_sem, out_sem,
):
    ctx, head, rep = lax.axis_index("ctx"), lax.axis_index("head"), lax.axis_index("rep")
    z, x = ctx // 2, ctx % 2
    me = ctx * 2 + rep
    mate = 15 - me
    late = me >= 8
    def shared(i):
        return i // 2 - 3 - jnp.where(i == 8, 1, 0)

    guests = jnp.where(late, 0, shared(mate))
    given = jnp.where(late, shared(me), 0)
    own_base = 1
    own_count = CHUNKS - given

    def place(dz, flip):
        return ((z + dz) % 4) * 2 + (1 - x if flip else x)

    chips = [ctx, place(0, True), place(1, False), place(3, False),
             place(1, True), place(3, True), place(2, False), place(2, True)]
    OWN, XP, ZP, ZM, ZPX, ZMX, ZZ, ZZX = range(8)

    sibling = {"ctx": ctx, "rep": 1 - rep}
    over_x = {"ctx": chips[XP], "rep": rep}
    over_zp = {"ctx": chips[ZP], "rep": rep}
    over_zm = {"ctx": chips[ZM], "rep": rep}
    to_mate = {"ctx": mate // 2, "rep": mate % 2}

    def load(src, dst, sem):
        copy = pltpu.make_async_copy(src, dst, sem)
        copy.start()
        return copy

    kv_in = load(kv_hbm, kvint, in_sem.at[0])
    dq_in = load(dq_hbm, qbuf.at[pl.ds(0, CHUNK)], in_sem.at[1])

    def own_q(k):
        return pltpu.make_async_copy(
            q_hbm.at[pl.ds(pl.multiple_of((given + k) * CHUNK, CHUNK), CHUNK)],
            qbuf.at[pl.ds(pl.multiple_of((own_base + k) * CHUNK, CHUNK), CHUNK)],
            q_sem.at[k],
        )

    for k in range(CHUNKS):
        @pl.when(k < own_count)
        def _(k=k):
            own_q(k).start()

    m_ref[...] = jnp.full(m_ref.shape, LOW_FILL, F32)
    l_ref[...] = jnp.zeros(l_ref.shape, F32)
    acc_ref[...] = jnp.zeros(acc_ref.shape, F32)

    tail_in = load(tail_hbm, tailbuf, in_sem.at[2])
    w_in = load(w_hbm, wbuf, in_sem.at[3])

    barrier = pltpu.get_barrier_semaphore()
    for device in (sibling, over_x, over_zp, over_zm, to_mate):
        pl.semaphore_signal(barrier, inc=1, device_id=device, device_id_type=MESH)
    for away in range(1, 8):
        pl.semaphore_signal(
            barrier, inc=1, device_id={"head": (head + away) % 8}, device_id_type=MESH
        )

    rows = lax.broadcasted_iota(jnp.int32, (256, 256), 0)
    cols = lax.broadcasted_iota(jnp.int32, (256, 256), 1)
    wanted = jnp.where(rows < 128, rows * 2, (rows - 128) * 2 + 1)
    pick = jnp.where(cols == wanted, 1.0, 0.0).astype(BF16)
    kv_in.wait()
    for t in range(4):
        apart = jnp.dot(pick, kvint[t * 256:(t + 1) * 256, :], preferred_element_type=F32)
        apart = apart.astype(BF16)
        here = pl.ds(pl.multiple_of(me * BLOCK + t * 128, 128), 128)
        kbuf[here, :] = apart[:128]
        vbuf[here, :] = apart[128:]

    pl.semaphore_wait(barrier, 12)

    sends = []

    def block_of(which, s, kind, piece):
        b = chips[s] * 2 + (rep if kind == 0 else 1 - rep)
        if which == "kv":
            ref = kbuf if piece == 0 else vbuf
            return ref.at[pl.ds(pl.multiple_of(b * BLOCK, BLOCK), BLOCK)]
        return att.at[pl.ds(pl.multiple_of(b * 64 + piece * 32, 32), 32)]

    def sem_of(which):
        return kv_sem if which == "kv" else att_sem

    def send(which, s, piece, device, s_there, kind_there):
        arguments = (which, s, piece, device, s_there, kind_there, len(sends))
        sends.append(arguments)
        sent(*arguments).start()

    def sent(which, s, piece, device, s_there, kind_there, number):
        return pltpu.make_async_remote_copy(
            src_ref=block_of(which, s, 0, piece),
            dst_ref=block_of(which, s, 0, piece),
            send_sem=send_sem.at[number],
            recv_sem=sem_of(which).at[s_there, kind_there, piece],
            device_id=device,
            device_id_type=MESH,
        )

    def arrived(which, s, kind, pieces=(0, 1)):
        for piece in pieces:
            ref = block_of(which, s, kind, piece)
            pltpu.make_async_remote_copy(
                src_ref=ref, dst_ref=ref, send_sem=send_sem.at[0],
                recv_sem=sem_of(which).at[s, kind, piece],
                device_id=sibling, device_id_type=MESH,
            ).wait_recv()

    def both(which, s, device, s_there, kind_there):
        for piece in (0, 1):
            send(which, s, piece, device, s_there, kind_there)

    def gather_start(which):
        both(which, OWN, over_zp, ZM, 0)
        both(which, OWN, over_zm, ZP, 0)
        both(which, OWN, over_x, XP, 0)
        both(which, OWN, sibling, OWN, 1)

    def gather_first(which):
        arrived(which, ZM, 0)
        send(which, ZM, 0, over_zp, ZZ, 0)
        arrived(which, ZP, 0)
        send(which, ZP, 1, over_zm, ZZ, 0)
        arrived(which, XP, 0)
        both(which, XP, over_zp, ZMX, 0)
        both(which, XP, over_zm, ZPX, 0)
        for s in (XP, ZM, ZP):
            both(which, s, sibling, s, 1)

    def gather_second(which):
        arrived(which, ZZ, 0)
        both(which, ZZ, over_x, ZZX, 0)
        both(which, ZZ, sibling, ZZ, 1)

    def gather_third(which):
        for s in (ZMX, ZPX, ZZX):
            arrived(which, s, 0)
            both(which, s, sibling, s, 1)

    gather_start("kv")

    def guest_q(k):
        return pltpu.make_async_remote_copy(
            src_ref=q_hbm.at[pl.ds(pl.multiple_of(k * CHUNK, CHUNK), CHUNK)],
            dst_ref=qbuf.at[pl.ds(pl.multiple_of((GUEST_BASE + k) * CHUNK, CHUNK), CHUNK)],
            send_sem=guest_sem.at[0, k], recv_sem=guest_sem.at[1, k],
            device_id=to_mate, device_id_type=MESH,
        )

    def rows_of(slot):
        return pl.ds(pl.multiple_of(slot * CHUNK, CHUNK), CHUNK)

    def absorb(slots, ranges, seen=None):
        where = [rows_of(slot) for slot in slots]
        keys = [pl.ds(pl.multiple_of(first, BLOCK), count) for first, count in ranges]
        old = [(m_ref[r, :], l_ref[r, :], acc_ref[r, :]) for r in where]
        scores = [
            [lax.dot_general(qbuf[r, :], kbuf[k, :], NT, preferred_element_type=F32) for k in keys]
            for r in where
        ]
        result = []
        for i, (m_old, l_old, a_old) in enumerate(old):
            parts = scores[i]
            if seen is not None:
                parts = [
                    jnp.concatenate(
                        [
                            jnp.where(
                                ahead[...] <= seen[i] - j * WIDTH,
                                s[:, j * WIDTH:(j + 1) * WIDTH],
                                LOW_FILL,
                            )
                            for j in range(s.shape[1] // WIDTH)
                        ],
                        axis=1,
                    )
                    for s in parts
                ]
            m_new = functools.reduce(
                jnp.maximum, [jnp.max(s, axis=1, keepdims=True) for s in parts], m_old
            )
            factor = jnp.exp2((m_old - m_new) * SCALE)
            total, mixed = l_old * factor, a_old * factor
            for s, k in zip(parts, keys):
                p = jnp.exp2((s - wide(m_new, s.shape[1])) * SCALE)
                for j in range(s.shape[1] // WIDTH):
                    total = total + p[:, j * WIDTH:(j + 1) * WIDTH]
                mixed = mixed + jnp.dot(p.astype(BF16), vbuf[k, :], preferred_element_type=F32)
            result.append((m_new, total, mixed))
        for i, r in enumerate(where):
            m_ref[r, :], l_ref[r, :], acc_ref[r, :] = result[i]

    def first_items(slot, pairs, who, place):
        blocks = who % 2 + 1

        def step(t, _):
            pair, b = t // blocks, t % blocks
            last = b == blocks - 1
            seen = [
                jnp.where(last, (place + 2 * pair + i) * 64, 2 * BLOCK) for i in range(2)
            ]
            absorb(
                [slot + 2 * pair, slot + 2 * pair + 1],
                [((who - blocks + 1 + b) * BLOCK, BLOCK)],
                seen,
            )
            return 0

        lax.fori_loop(0, pairs * blocks, step, 0)

    def half_items(slot, count, who):
        def step(k, _):
            absorb([slot + k], [(who // 4 * 4 * BLOCK, 2 * BLOCK)])
            return 0

        lax.fori_loop(0, jnp.where(who // 2 % 2 == 1, count, 0), step, 0)

    def pick_chip(k, group):
        return functools.reduce(
            lambda rest, n: jnp.where(k == n, chips[group[n]], rest),
            range(1, len(group)),
            chips[group[0]],
        )

    def decode_items(first, second):
        def step(k, _):
            where = (pick_chip(k, first), pick_chip(k, second))
            absorb([0], [(chip * 2 * BLOCK, 2 * BLOCK) for chip in where])
            return 0

        lax.fori_loop(0, 2, step, 0)

    def finish(slot):
        r = rows_of(slot)
        obuf[r, :] = (
            acc_ref[r, :] / jnp.sum(l_ref[r, :], axis=1, keepdims=True)
        ).astype(BF16)

    def own_out(k):
        return pltpu.make_async_copy(
            obuf.at[pl.ds(pl.multiple_of((own_base + k) * CHUNK, CHUNK), CHUNK)],
            out_hbm.at[pl.ds(pl.multiple_of((given + k) * CHUNK, CHUNK), CHUNK)],
            out_sem.at[k],
        )

    def give(lo, hi):
        for k in range(lo, hi):
            @pl.when(k < given)
            def _(k=k):
                guest_q(k).start()

    ahead[...] = (
        lax.broadcasted_iota(jnp.int32, (CHUNK, WIDTH), 1)
        - lax.broadcasted_iota(jnp.int32, (CHUNK, WIDTH), 0) // 8
    )

    dq_in.wait()
    tail_in.wait()

    def tail_step(t, _):
        first = t * ROLLS
        scores, kv = [], []
        col = lax.broadcasted_iota(jnp.int32, (8, 256), 1)
        even = jnp.where(col % 2 == 0, col, 512)
        for u in range(ROLLS):
            r = first + u
            kv.append(pl.ds(pl.multiple_of(r * 256, 256), 256))
            q16 = qbuf[pl.ds(pl.multiple_of((first + u // 2 * 2) * 8, 16), 16), :]
            s = lax.dot_general(q16, tailbuf[kv[u], :], NT, preferred_element_type=F32)
            s = s[u % 2 * 8:u % 2 * 8 + 8]
            scores.append(jnp.where(even < 2 * len_ref[r], s, LOW_FILL))
        s = jnp.concatenate(scores, axis=0)
        m_new = jnp.broadcast_to(jnp.max(s, axis=1, keepdims=True), (8 * ROLLS, WIDTH))
        p = jnp.exp2((s - wide(m_new, 256)) * SCALE)
        here = pl.ds(pl.multiple_of(t * 8 * ROLLS, 8 * ROLLS), 8 * ROLLS)
        m_ref[here, :] = m_new
        l_ref[here, :] = p[:, :WIDTH] + p[:, WIDTH:]
        p = pltpu.roll(p, 1, 1).astype(BF16)
        out = []
        for u in range(ROLLS):
            p16 = p[u // 2 * 16:u // 2 * 16 + 16]
            o = jnp.dot(p16, tailbuf[kv[u], :], preferred_element_type=F32)
            out.append(o[u % 2 * 8:u % 2 * 8 + 8])
        acc_ref[here, :] = jnp.concatenate(out, axis=0)
        return 0

    lax.fori_loop(0, 64 // ROLLS, tail_step, 0)

    gather_first("kv")
    arrived("kv", OWN, 1)
    for k in range(CHUNKS):
        @pl.when(k < own_count)
        def _(k=k):
            own_q(k).wait()

    own_pairs = (own_count + 1) // 2
    first_items(own_base, own_pairs, me, given)
    gather_second("kv")
    give(0, EARLY)
    for s in (XP, ZM, ZP):
        arrived("kv", s, 1)
    decode_items((OWN, ZM), (XP, ZP))
    gather_third("kv")
    give(EARLY, GUESTS)
    for s in (ZZ, ZMX, ZPX, ZZX):
        arrived("kv", s, 1)
    decode_items((ZZ, ZPX), (ZMX, ZZX))

    total = jnp.sum(l_ref[:CHUNK, :], axis=1, keepdims=True)
    fbuf[...] = acc_ref[:CHUNK, :] / total
    mine = pl.ds(pl.multiple_of(me * 64, 64), 64)
    for h in range(8):
        att[mine, h * WIDTH:(h + 1) * WIDTH] = fbuf[pl.ds(h, 64, stride=8), :].astype(BF16)
    gather_start("att")

    def rs_copy(chip, number):
        return pltpu.make_async_remote_copy(
            src_ref=part.at[pl.ds(pl.multiple_of(chip * 128, 128), 128)],
            dst_ref=landed.at[pl.ds(pl.multiple_of(head * 128, 128), 128)],
            send_sem=rs_sem.at[0, number], recv_sem=rs_sem.at[1, head],
            device_id={"head": chip}, device_id_type=MESH,
        )

    def project(chip):
        rows_here = pl.ds(pl.multiple_of(chip * 128, 128), 128)
        part[rows_here, :] = jnp.dot(
            att[rows_here, :], wbuf[...], preferred_element_type=F32
        ).astype(BF16)

        @pl.when(chip != head)
        def _():
            rs_copy(chip, chip).start()

    def give_back(k):
        return pltpu.make_async_remote_copy(
            src_ref=obuf.at[pl.ds(pl.multiple_of((GUEST_BASE + k) * CHUNK, CHUNK), CHUNK)],
            dst_ref=out_hbm.at[pl.ds(pl.multiple_of(k * CHUNK, CHUNK), CHUNK)],
            send_sem=back_sem.at[0, k], recv_sem=back_sem.at[1, k],
            device_id=to_mate, device_id_type=MESH,
        )

    def projects(group):
        def step(k, _):
            project(pick_chip(k, group))
            return 0

        lax.fori_loop(0, len(group), step, 0)

    guest_planes = mate // 4
    guest_items = guests * guest_planes
    items = guest_items + own_count * z

    def plane_items(lo, hi):
        def step(t, _):
            foreign = t < guest_items
            after = jnp.where(foreign, t, t - guest_items)
            planes = jnp.maximum(jnp.where(foreign, guest_planes, z), 1)
            k, j = after // planes, after % planes
            slot = jnp.where(foreign, GUEST_BASE, own_base) + k
            absorb([slot], [(j * 4 * BLOCK, 4 * BLOCK)])

            @pl.when(j == planes - 1)
            def _():
                finish(slot)

                @pl.when(foreign)
                def _():
                    give_back(k).start()

                @pl.when(jnp.logical_not(foreign))
                def _():
                    own_out(k).start()

            return 0

        lax.fori_loop(lo, jnp.minimum(hi, items), step, 0)

    half_items(own_base, own_count, me)

    @pl.when(z == 0)
    def _():
        def step(k, _):
            finish(own_base + k)
            own_out(k).start()
            return 0

        lax.fori_loop(0, own_count, step, 0)

    gather_first("att")

    def guest_in(k, _):
        guest_q(k).wait_recv()
        return 0

    lax.fori_loop(0, guests, guest_in, 0)
    first_items(GUEST_BASE, (guests + 1) // 2, mate, 0)
    gather_second("att")
    half_items(GUEST_BASE, guests, mate)
    w_in.wait()
    for s in (OWN, XP, ZM, ZP):
        arrived("att", s, 1)
    projects((OWN, XP, ZM, ZP))
    plane_items(0, ITEMS[0])
    gather_third("att")
    plane_items(ITEMS[0], ITEMS[1])
    for s in (ZZ, ZMX, ZPX, ZZX):
        arrived("att", s, 1)
    projects((ZZ, ZMX, ZPX, ZZX))
    plane_items(ITEMS[1], 1000)

    own_part = pltpu.make_async_copy(
        part.at[pl.ds(pl.multiple_of(head * 128, 128), 128)],
        landed.at[pl.ds(pl.multiple_of(head * 128, 128), 128)],
        in_sem.at[0],
    )
    own_part.start()
    own_part.wait()
    for away in range(1, 8):
        other = (head + away) % 8
        there = landed.at[pl.ds(pl.multiple_of(other * 128, 128), 128)]
        pltpu.make_async_remote_copy(
            src_ref=there, dst_ref=there, send_sem=rs_sem.at[0, 0],
            recv_sem=rs_sem.at[1, other], device_id={"head": other}, device_id_type=MESH,
        ).wait_recv()

    for arguments in sends:
        sent(*arguments).wait_send()
    for k in range(1, 8):
        rs_copy((head + k) % 8, (head + k) % 8).wait_send()
    for k in range(GUESTS):
        @pl.when(k < given)
        def _(k=k):
            guest_q(k).wait_send()
            give_back(k).wait_recv()

        @pl.when(k < guests)
        def _(k=k):
            give_back(k).wait_send()
    for k in range(CHUNKS):
        @pl.when(k < own_count)
        def _(k=k):
            own_out(k).wait()


def last_kernel(rows_hbm, parts_hbm, out_hbm, dec_ref, parts, row_sem, part_sem):
    copies = []
    for k in range(8):
        here = pl.ds(k * 128, 128)
        copies.append(pltpu.make_async_copy(parts_hbm.at[here], parts.at[here], part_sem.at[k]))
    for k in range(8):
        here = pl.ds(k * CHUNK, CHUNK)
        copies.append(pltpu.make_async_copy(rows_hbm.at[here], out_hbm.at[here], row_sem.at[k]))
    for copy in copies:
        copy.start()
    total = jnp.zeros((128, 512), F32)
    for k in range(8):
        copies[k].wait()
        total = total + parts[k * 128:(k + 1) * 128, :].astype(F32)
    dec_ref[...] = total.astype(BF16)
    for copy in copies[8:]:
        copy.wait()


def on_device(prefix_query, prefix_kv, decode_query, tail_key_value, tail_len, out_weight):
    any_space = pl.BlockSpec(memory_space=pl.ANY)
    rows_out, parts = pl.pallas_call(
        kernel,
        out_shape=(
            jax.ShapeDtypeStruct((CHUNKS * CHUNK, WIDTH), BF16),
            jax.ShapeDtypeStruct((1024, 512), BF16),
        ),
        in_specs=[any_space] * 4 + [pl.BlockSpec(memory_space=pltpu.SMEM), any_space],
        out_specs=(any_space, any_space),
        scratch_shapes=[
            pltpu.VMEM((2 * BLOCK, WIDTH), BF16),
            pltpu.VMEM((16 * BLOCK, WIDTH), BF16),
            pltpu.VMEM((16 * BLOCK, WIDTH), BF16),
            pltpu.VMEM((SLOTS * CHUNK, WIDTH), BF16),
            pltpu.VMEM((64 * 256, WIDTH), BF16),
            pltpu.VMEM((1024, 512), BF16),
            pltpu.VMEM((SLOTS * CHUNK, WIDTH), F32),
            pltpu.VMEM((SLOTS * CHUNK, WIDTH), F32),
            pltpu.VMEM((SLOTS * CHUNK, WIDTH), F32),
            pltpu.VMEM((SLOTS * CHUNK, WIDTH), BF16),
            pltpu.VMEM((CHUNK, WIDTH), F32),
            pltpu.VMEM((CHUNK, WIDTH), jnp.int32),
            pltpu.VMEM((1024, 1024), BF16),
            pltpu.VMEM((1024, 512), BF16),
            pltpu.SemaphoreType.DMA((4,)),
            pltpu.SemaphoreType.DMA((CHUNKS,)),
            pltpu.SemaphoreType.DMA((64,)),
            pltpu.SemaphoreType.DMA((8, 2, 2)),
            pltpu.SemaphoreType.DMA((8, 2, 2)),
            pltpu.SemaphoreType.DMA((2, GUESTS)),
            pltpu.SemaphoreType.DMA((2, GUESTS)),
            pltpu.SemaphoreType.DMA((2, 8)),
            pltpu.SemaphoreType.DMA((CHUNKS,)),
        ],
        compiler_params=pltpu.CompilerParams(
            collective_id=0, has_side_effects=True, vmem_limit_bytes=56 << 20
        ),
        name="layer_attention",
    )(
        prefix_query.reshape(CHUNKS * CHUNK, WIDTH),
        prefix_kv.reshape(2 * BLOCK, WIDTH),
        decode_query.reshape(CHUNK, WIDTH),
        tail_key_value.reshape(64 * 256, WIDTH),
        tail_len,
        out_weight,
    )
    prefix_out, decoded = pl.pallas_call(
        last_kernel,
        out_shape=(
            jax.ShapeDtypeStruct((CHUNKS * CHUNK, WIDTH), BF16),
            jax.ShapeDtypeStruct((128, 512), BF16),
        ),
        in_specs=[any_space] * 2,
        out_specs=(any_space, pl.BlockSpec(memory_space=pltpu.VMEM)),
        scratch_shapes=[
            pltpu.VMEM((1024, 512), BF16),
            pltpu.SemaphoreType.DMA((8,)),
            pltpu.SemaphoreType.DMA((8,)),
        ],
        compiler_params=pltpu.CompilerParams(vmem_limit_bytes=8 << 20),
        name="results",
    )(rows_out, parts)
    return prefix_out.reshape(prefix_query.shape), decoded


def solution(mesh):
    return jax.shard_map(
        on_device,
        mesh=mesh,
        in_specs=(
            P(("ctx", "rep"), "head", None),
            P(("ctx", "rep"), "head", None, None),
            P(("ctx", "rep"), "head", None),
            P(("ctx", "rep"), None, "head", None, None),
            P(("ctx", "rep")),
            P("head", ("ctx", "rep")),
        ),
        out_specs=(P(("ctx", "rep"), "head", None), P("head", ("ctx", "rep"))),
        check_vma=False,
    )
```

time: 95.9 us -> 85.2 us (0.89)
  Pallas kernels: 90.1 us -> 81 us
  local copies, waits for them, and re-layouts: 3.83 us -> 2.44 us
    pallas_call x1, Pallas kernels: 90.1 us -> 78 us  [on_device(): pl.pallas_call(kernel, out_shape=(jax.ShapeDtypeStruct((CHUNKS * CHUNK, W...]
    pallas_call x0 -> x1, Pallas kernels: none -> 3.07 us  [on_device(): pl.pallas_call(last_kernel, out_shape=(jax.ShapeDtypeStruct((CHUNKS * CHU...]
    unnamed x2 -> x4, local copies, waits for them, and re-layouts: 3.83 us -> 2.44 us
where the time goes in v2:
time: 85.2 us; the launch traced here: 84.3 us
  Pallas kernels  81 us (95%)
  local copies, waits for them, and re-layouts  2.44 us (3%)
    pallas_call x1, Pallas kernels, on_device(): pl.pallas_call(kernel, out_shape=(jax.ShapeDtypeStruct((CHUNKS * CHUNK, W...  78 us
    pallas_call x1, Pallas kernels, on_device(): pl.pallas_call(last_kernel, out_shape=(jax.ShapeDtypeStruct((CHUNKS * CHU...  3.07 us
    unnamed x4, local copies, waits for them, and re-layouts  2.44 us

profile of v2, /device:TPU:99, one launch (start us, length us, event | category | flops | bytes accessed | tf_op | source)
XLA Modules:
  0.0 84.3 jit_solution(16551734120450090202)
XLA Ops:
  0.6 78.0 %layer_attention.1 = (bf16[4096,128]{1,0:T(8,128)(2,1)}, bf16[1024,512]{1,0:T(8,128)(2,1)}) custom-call(bf16[4096,128]{1,0:T(8,128)(2,1)} %bitcast.6, bf16[1024,128]{1,0:T(8,128)(2,1)} %bitcast.7, bf16[512,128]{1,0:T(8,128)(2,1)} %bitcast.8, bf16[16384,128]{1,0:T(8,128)(2,1)} %bitcast.5, s32[64]{0:T(128)} %len_ref.1, bf16[1024,512]{1,0:T(8,128)(2,1)} %w_hbm.1), custom_call_target="tpu_custom_call" | custom-call | tf_op jit(solution)/shard_map/layer_attention/pallas_call | solution.py:506
  78.6 0.0 copy-start
  78.6 1.2 %copy-done = bf16[4096,128]{1,0:T(8,128)(2,1)S(1)} copy-done((bf16[4096,128]{1,0:T(8,128)(2,1)S(1)}, bf16[4096,128]{1,0:T(8,128)(2,1)}, u32[]{:S(2)}) %copy-start) | copy-done | bytes 1048600
  79.8 0.0 copy-start.1
  79.8 1.2 %copy-done.1 = bf16[1024,512]{1,0:T(8,128)(2,1)S(1)} copy-done((bf16[1024,512]{1,0:T(8,128)(2,1)S(1)}, bf16[1024,512]{1,0:T(8,128)(2,1)}, u32[]{:S(2)}) %copy-start.1) | copy-done | bytes 1048600
  81.1 3.1 %results.1 = (bf16[4096,128]{1,0:T(8,128)(2,1)}, bf16[128,512]{1,0:T(8,128)(2,1)}) custom-call(bf16[4096,128]{1,0:T(8,128)(2,1)S(1)} %copy-done, bf16[1024,512]{1,0:T(8,128)(2,1)S(1)} %copy-done.1), custom_call_target="tpu_custom_call" | custom-call | tf_op jit(solution)/shard_map/results/pallas_call | solution.py:551
Async XLA Ops:
  78.6 1.2 %copy-start = (bf16[4096,128]{1,0:T(8,128)(2,1)S(1)}, bf16[4096,128]{1,0:T(8,128)(2,1)}, u32[]{:S(2)}) copy-start(bf16[4096,128]{1,0:T(8,128)(2,1)} %get-tuple-element.6.rows_hbm) | copy-start | bytes 3145732
  79.8 1.2 %copy-start.1 = (bf16[1024,512]{1,0:T(8,128)(2,1)S(1)}, bf16[1024,512]{1,0:T(8,128)(2,1)}, u32[]{:S(2)}) copy-start(bf16[1024,512]{1,0:T(8,128)(2,1)} %get-tuple-element.7.parts_hbm) | copy-start | bytes 3145732

commit v3 on v2

--- a/solution.py
+++ b/solution.py
@@ -21,7 +21,8 @@
 NT = (((1,), (1,)), ((), ()))
 EARLY = 1
 ROLLS = 16
-ITEMS = (3, 4)
+CHIP_ITEMS = (1, 2, 2, 1, 1)
+PLANE_ITEMS = (1, 3)
 
 
 def wide(column, width):
@@ -41,7 +42,7 @@
     mate = 15 - me
     late = me >= 8
     def shared(i):
-        return i // 2 - 3 - jnp.where(i == 8, 1, 0)
+        return (i - 7) * 7 // 16
 
     guests = jnp.where(late, 0, shared(mate))
     given = jnp.where(late, shared(me), 0)
@@ -60,33 +61,6 @@
     over_zp = {"ctx": chips[ZP], "rep": rep}
     over_zm = {"ctx": chips[ZM], "rep": rep}
     to_mate = {"ctx": mate // 2, "rep": mate % 2}
-
-    def load(src, dst, sem):
-        copy = pltpu.make_async_copy(src, dst, sem)
-        copy.start()
-        return copy
-
-    kv_in = load(kv_hbm, kvint, in_sem.at[0])
-    dq_in = load(dq_hbm, qbuf.at[pl.ds(0, CHUNK)], in_sem.at[1])
-
-    def own_q(k):
-        return pltpu.make_async_copy(
-            q_hbm.at[pl.ds(pl.multiple_of((given + k) * CHUNK, CHUNK), CHUNK)],
-            qbuf.at[pl.ds(pl.multiple_of((own_base + k) * CHUNK, CHUNK), CHUNK)],
-            q_sem.at[k],
-        )
-
-    for k in range(CHUNKS):
-        @pl.when(k < own_count)
-        def _(k=k):
-            own_q(k).start()
-
-    m_ref[...] = jnp.full(m_ref.shape, LOW_FILL, F32)
-    l_ref[...] = jnp.zeros(l_ref.shape, F32)
-    acc_ref[...] = jnp.zeros(acc_ref.shape, F32)
-
-    tail_in = load(tail_hbm, tailbuf, in_sem.at[2])
-    w_in = load(w_hbm, wbuf, in_sem.at[3])
 
     barrier = pltpu.get_barrier_semaphore()
     for device in (sibling, over_x, over_zp, over_zm, to_mate):
@@ -95,6 +69,29 @@
         pl.semaphore_signal(
             barrier, inc=1, device_id={"head": (head + away) % 8}, device_id_type=MESH
         )
+
+    def load(src, dst, sem):
+        copy = pltpu.make_async_copy(src, dst, sem)
+        copy.start()
+        return copy
+
+    kv_in = load(kv_hbm, kvint, in_sem.at[0])
+    dq_in = load(dq_hbm, qbuf.at[pl.ds(0, CHUNK)], in_sem.at[1])
+
+    def own_q(k):
+        return pltpu.make_async_copy(
+            q_hbm.at[pl.ds(pl.multiple_of((given + k) * CHUNK, CHUNK), CHUNK)],
+            qbuf.at[pl.ds(pl.multiple_of((own_base + k) * CHUNK, CHUNK), CHUNK)],
+            q_sem.at[k],
+        )
+
+    for k in range(CHUNKS):
+        @pl.when(k < own_count)
+        def _(k=k):
+            own_q(k).start()
+
+    tail_in = load(tail_hbm, tailbuf, in_sem.at[2])
+    w_in = load(w_hbm, wbuf, in_sem.at[3])
 
     rows = lax.broadcasted_iota(jnp.int32, (256, 256), 0)
     cols = lax.broadcasted_iota(jnp.int32, (256, 256), 1)
@@ -108,6 +105,13 @@
         kbuf[here, :] = apart[:128]
         vbuf[here, :] = apart[128:]
 
+    m_ref[...] = jnp.full(m_ref.shape, LOW_FILL, F32)
+    l_ref[...] = jnp.zeros(l_ref.shape, F32)
+    acc_ref[...] = jnp.zeros(acc_ref.shape, F32)
+    ahead[...] = (
+        lax.broadcasted_iota(jnp.int32, (CHUNK, WIDTH), 1)
+        - lax.broadcasted_iota(jnp.int32, (CHUNK, WIDTH), 0) // 8
+    )
     pl.semaphore_wait(barrier, 12)
 
     sends = []
@@ -230,7 +234,7 @@
         for i, r in enumerate(where):
             m_ref[r, :], l_ref[r, :], acc_ref[r, :] = result[i]
 
-    def first_items(slot, pairs, who, place):
+    def first_items(slot, lo, hi, who, place):
         blocks = who % 2 + 1
 
         def step(t, _):
@@ -246,14 +250,32 @@
             )
             return 0
 
-        lax.fori_loop(0, pairs * blocks, step, 0)
-
-    def half_items(slot, count, who):
+        lax.fori_loop(lo * blocks, hi * blocks, step, 0)
+
+    def half_items(slot, lo, hi, who):
         def step(k, _):
             absorb([slot + k], [(who // 4 * 4 * BLOCK, 2 * BLOCK)])
             return 0
 
-        lax.fori_loop(0, jnp.where(who // 2 % 2 == 1, count, 0), step, 0)
+        lax.fori_loop(lo, jnp.where(who // 2 % 2 == 1, hi, lo), step, 0)
+
+    before = jnp.where(z > 0, 1, 0)
+    own_pairs = (own_count + 1) // 2
+    chip_early = own_pairs * (x + before)
+    chip_all = chip_early + own_pairs * before
+
+    def chip_items(lo, hi):
+        def step(t, _):
+            b, k = t // own_pairs, t % own_pairs
+            chip = jnp.where(
+                jnp.logical_and(x == 1, b == 0),
+                chips[XP],
+                jnp.where(b == x, chips[ZM], chips[ZMX]),
+            )
+            absorb([own_base + 2 * k, own_base + 2 * k + 1], [(chip * 2 * BLOCK, 2 * BLOCK)])
+            return 0
+
+        lax.fori_loop(lo, hi, step, 0)
 
     def pick_chip(k, group):
         return functools.reduce(
@@ -288,11 +310,6 @@
             @pl.when(k < given)
             def _(k=k):
                 guest_q(k).start()
-
-    ahead[...] = (
-        lax.broadcasted_iota(jnp.int32, (CHUNK, WIDTH), 1)
-        - lax.broadcasted_iota(jnp.int32, (CHUNK, WIDTH), 0) // 8
-    )
 
     dq_in.wait()
     tail_in.wait()
@@ -326,20 +343,22 @@
 
     lax.fori_loop(0, 64 // ROLLS, tail_step, 0)
 
-    gather_first("kv")
     arrived("kv", OWN, 1)
     for k in range(CHUNKS):
         @pl.when(k < own_count)
         def _(k=k):
             own_q(k).wait()
 
-    own_pairs = (own_count + 1) // 2
-    first_items(own_base, own_pairs, me, given)
+    first_items(own_base, 0, 2, me, given)
+    gather_first("kv")
+    first_items(own_base, 2, own_pairs, me, given)
     gather_second("kv")
     give(0, EARLY)
     for s in (XP, ZM, ZP):
         arrived("kv", s, 1)
     decode_items((OWN, ZM), (XP, ZP))
+    chip_done = jnp.minimum(chip_early, CHIP_ITEMS[0])
+    chip_items(0, chip_done)
     gather_third("kv")
     give(EARLY, GUESTS)
     for s in (ZZ, ZMX, ZPX, ZZX):
@@ -386,15 +405,15 @@
 
         lax.fori_loop(0, len(group), step, 0)
 
-    guest_planes = mate // 4
+    guest_planes, own_planes = mate // 4, jnp.maximum(z - 1, 0)
     guest_items = guests * guest_planes
-    items = guest_items + own_count * z
+    items = guest_items + own_count * own_planes
 
     def plane_items(lo, hi):
         def step(t, _):
             foreign = t < guest_items
             after = jnp.where(foreign, t, t - guest_items)
-            planes = jnp.maximum(jnp.where(foreign, guest_planes, z), 1)
+            planes = jnp.maximum(jnp.where(foreign, guest_planes, own_planes), 1)
             k, j = after // planes, after % planes
             slot = jnp.where(foreign, GUEST_BASE, own_base) + k
             absorb([slot], [(j * 4 * BLOCK, 4 * BLOCK)])
@@ -413,11 +432,48 @@
 
             return 0
 
-        lax.fori_loop(lo, jnp.minimum(hi, items), step, 0)
-
-    half_items(own_base, own_count, me)
-
-    @pl.when(z == 0)
+        lax.fori_loop(lo, hi, step, 0)
+
+    w_in.wait()
+    chip_next = jnp.minimum(chip_done + CHIP_ITEMS[1], chip_all)
+    chip_items(chip_done, chip_next)
+    arrived("att", OWN, 1)
+    project(ctx)
+    gather_first("att")
+
+    def guest_in(k, _):
+        guest_q(k).wait_recv()
+        return 0
+
+    def guests_in(lo, hi):
+        hi = jnp.minimum(hi, guests)
+        lax.fori_loop(lo, hi, guest_in, 0)
+        first_items(GUEST_BASE, lo // 2, (hi + 1) // 2, mate, 0)
+        half_items(GUEST_BASE, lo, hi, mate)
+
+    guests_in(0, 2)
+    chip_last = jnp.minimum(chip_next + CHIP_ITEMS[2], chip_all)
+    chip_items(chip_next, chip_last)
+    gather_second("att")
+    for s in (XP, ZM, ZP):
+        arrived("att", s, 1)
+    projects((XP, ZM, ZP))
+    chip_more = jnp.minimum(chip_last + CHIP_ITEMS[3], chip_all)
+    chip_items(chip_last, chip_more)
+    plane_done = jnp.minimum(guest_items, PLANE_ITEMS[0])
+    plane_items(0, plane_done)
+    gather_third("att")
+    chip_most = jnp.minimum(chip_more + CHIP_ITEMS[4], chip_all)
+    chip_items(chip_more, chip_most)
+    plane_next = jnp.minimum(guest_items, PLANE_ITEMS[1])
+    plane_items(plane_done, plane_next)
+    for s in (ZZ, ZMX, ZPX, ZZX):
+        arrived("att", s, 1)
+    projects((ZZ, ZMX, ZPX, ZZX))
+    guests_in(2, GUESTS)
+    chip_items(chip_most, chip_all)
+
+    @pl.when(z < 2)
     def _():
         def step(k, _):
             finish(own_base + k)
@@ -426,27 +482,7 @@
 
         lax.fori_loop(0, own_count, step, 0)
 
-    gather_first("att")
-
-    def guest_in(k, _):
-        guest_q(k).wait_recv()
-        return 0
-
-    lax.fori_loop(0, guests, guest_in, 0)
-    first_items(GUEST_BASE, (guests + 1) // 2, mate, 0)
-    gather_second("att")
-    half_items(GUEST_BASE, guests, mate)
-    w_in.wait()
-    for s in (OWN, XP, ZM, ZP):
-        arrived("att", s, 1)
-    projects((OWN, XP, ZM, ZP))
-    plane_items(0, ITEMS[0])
-    gather_third("att")
-    plane_items(ITEMS[0], ITEMS[1])
-    for s in (ZZ, ZMX, ZPX, ZZX):
-        arrived("att", s, 1)
-    projects((ZZ, ZMX, ZPX, ZZX))
-    plane_items(ITEMS[1], 1000)
+    plane_items(plane_next, items)
 
     own_part = pltpu.make_async_copy(
         part.at[pl.ds(pl.multiple_of(head * 128, 128), 128)],
@@ -482,22 +518,39 @@
             own_out(k).wait()
 
 
-def last_kernel(rows_hbm, parts_hbm, out_hbm, dec_ref, parts, row_sem, part_sem):
-    copies = []
-    for k in range(8):
-        here = pl.ds(k * 128, 128)
-        copies.append(pltpu.make_async_copy(parts_hbm.at[here], parts.at[here], part_sem.at[k]))
-    for k in range(8):
-        here = pl.ds(k * CHUNK, CHUNK)
-        copies.append(pltpu.make_async_copy(rows_hbm.at[here], out_hbm.at[here], row_sem.at[k]))
-    for copy in copies:
+def last_kernel(rows_hbm, parts_hbm, out_hbm, dec_ref, rows, parts, row_sem, part_sem, out_sem):
+    def here(k, count):
+        return pl.ds(k * count, count)
+
+    loads = [
+        pltpu.make_async_copy(
+            rows_hbm.at[here(k, CHUNK)], rows.at[here(k, CHUNK)], row_sem.at[k]
+        )
+        for k in range(8)
+    ]
+    adds = [
+        pltpu.make_async_copy(
+            parts_hbm.at[here(k, 128)], parts.at[here(k, 128)], part_sem.at[k]
+        )
+        for k in range(8)
+    ]
+    stores = [
+        pltpu.make_async_copy(
+            rows.at[here(k, CHUNK)], out_hbm.at[here(k, CHUNK)], out_sem.at[k]
+        )
+        for k in range(8)
+    ]
+    for copy in adds + loads:
         copy.start()
     total = jnp.zeros((128, 512), F32)
     for k in range(8):
-        copies[k].wait()
+        adds[k].wait()
         total = total + parts[k * 128:(k + 1) * 128, :].astype(F32)
     dec_ref[...] = total.astype(BF16)
-    for copy in copies[8:]:
+    for k in range(8):
+        loads[k].wait()
+        stores[k].start()
+    for copy in stores:
         copy.wait()
 
 
@@ -554,14 +607,16 @@
             jax.ShapeDtypeStruct((CHUNKS * CHUNK, WIDTH), BF16),
             jax.ShapeDtypeStruct((128, 512), BF16),
         ),
-        in_specs=[any_space] * 2,
-        out_specs=(any_space, pl.BlockSpec(memory_space=pltpu.VMEM)),
+        in_specs=[pl.BlockSpec(memory_space=pltpu.HBM)] * 2,
+        out_specs=(pl.BlockSpec(memory_space=pltpu.HBM), pl.BlockSpec(memory_space=pltpu.VMEM)),
         scratch_shapes=[
+            pltpu.VMEM((CHUNKS * CHUNK, WIDTH), BF16),
             pltpu.VMEM((1024, 512), BF16),
             pltpu.SemaphoreType.DMA((8,)),
             pltpu.SemaphoreType.DMA((8,)),
+            pltpu.SemaphoreType.DMA((8,)),
         ],
-        compiler_params=pltpu.CompilerParams(vmem_limit_bytes=8 << 20),
+        compiler_params=pltpu.CompilerParams(vmem_limit_bytes=56 << 20),
         name="results",
     )(rows_out, parts)
     return prefix_out.reshape(prefix_query.shape), decoded

time: 85.2 us -> 76.3 us (0.90)
  Pallas kernels: 81 us -> 74.2 us
  local copies, waits for them, and re-layouts: 2.44 us -> 0 us
    pallas_call x1, Pallas kernels: 78 us -> 70.8 us  [on_device(): pl.pallas_call(kernel, out_shape=(jax.ShapeDtypeStruct((CHUNKS * CHUNK, W...]
    unnamed x4 -> x0, local copies, waits for them, and re-layouts: 2.44 us -> none
where the time goes in v3:
time: 76.3 us; the launch traced here: 75.1 us
  Pallas kernels  74.2 us (97%)
  between operations  0.82 us (1%)
    pallas_call x1, Pallas kernels, on_device(): pl.pallas_call(kernel, out_shape=(jax.ShapeDtypeStruct((CHUNKS * CHUNK, W...  70.8 us
    pallas_call x1, Pallas kernels, on_device(): pl.pallas_call(last_kernel, out_shape=(jax.ShapeDtypeStruct((CHUNKS * CHU...  3.4 us

profile of v3, /device:TPU:99, one launch (start us, length us, event | category | flops | bytes accessed | tf_op | source)
XLA Modules:
  0.0 75.1 jit_solution(2328856771113022030)
XLA Ops:
  0.6 70.8 %layer_attention.1 = (bf16[4096,128]{1,0:T(8,128)(2,1)}, bf16[1024,512]{1,0:T(8,128)(2,1)}) custom-call(bf16[4096,128]{1,0:T(8,128)(2,1)} %bitcast.6, bf16[1024,128]{1,0:T(8,128)(2,1)} %bitcast.7, bf16[512,128]{1,0:T(8,128)(2,1)} %bitcast.8, bf16[16384,128]{1,0:T(8,128)(2,1)} %bitcast.5, s32[64]{0:T(128)} %len_ref.1, bf16[1024,512]{1,0:T(8,128)(2,1)} %w_hbm.1), custom_call_target="tpu_custom_call" | custom-call | tf_op jit(solution)/shard_map/layer_attention/pallas_call | solution.py:559
  71.5 3.4 %results.1 = (bf16[4096,128]{1,0:T(8,128)(2,1)}, bf16[128,512]{1,0:T(8,128)(2,1)}) custom-call(bf16[4096,128]{1,0:T(8,128)(2,1)} %get-tuple-element.6.rows_hbm, bf16[1024,512]{1,0:T(8,128)(2,1)} %get-tuple-element.7.parts_hbm), custom_call_target="tpu_custom_call" | custom-call | tf_op jit(solution)/shard_map/results/pallas_call | solution.py:604

commit v4 on v3

--- a/solution.py
+++ b/solution.py
@@ -349,9 +349,9 @@
         def _(k=k):
             own_q(k).wait()
 
-    first_items(own_base, 0, 2, me, given)
+    first_items(own_base, 0, 1, me, given)
     gather_first("kv")
-    first_items(own_base, 2, own_pairs, me, given)
+    first_items(own_base, 1, own_pairs, me, given)
     gather_second("kv")
     give(0, EARLY)
     for s in (XP, ZM, ZP):

time: 76.3 us -> 75.8 us (level)
  no operation moved by 1% of the time
where the time goes in v4:
time: 75.8 us; the launch traced here: 75.2 us
  Pallas kernels  74.4 us (98%)
  between operations  0.82 us (1%)
    pallas_call x1, Pallas kernels, on_device(): pl.pallas_call(kernel, out_shape=(jax.ShapeDtypeStruct((CHUNKS * CHUNK, W...  71 us
    pallas_call x1, Pallas kernels, on_device(): pl.pallas_call(last_kernel, out_shape=(jax.ShapeDtypeStruct((CHUNKS * CHU...  3.4 us

profile of v4, /device:TPU:99, one launch (start us, length us, event | category | flops | bytes accessed | tf_op | source)
XLA Modules:
  0.0 75.2 jit_solution(5557901093939337467)
XLA Ops:
  0.6 71.0 %layer_attention.1 = (bf16[4096,128]{1,0:T(8,128)(2,1)}, bf16[1024,512]{1,0:T(8,128)(2,1)}) custom-call(bf16[4096,128]{1,0:T(8,128)(2,1)} %bitcast.6, bf16[1024,128]{1,0:T(8,128)(2,1)} %bitcast.7, bf16[512,128]{1,0:T(8,128)(2,1)} %bitcast.8, bf16[16384,128]{1,0:T(8,128)(2,1)} %bitcast.5, s32[64]{0:T(128)} %len_ref.1, bf16[1024,512]{1,0:T(8,128)(2,1)} %w_hbm.1), custom_call_target="tpu_custom_call" | custom-call | tf_op jit(solution)/shard_map/layer_attention/pallas_call | solution.py:559
  71.6 3.4 %results.1 = (bf16[4096,128]{1,0:T(8,128)(2,1)}, bf16[128,512]{1,0:T(8,128)(2,1)}) custom-call(bf16[4096,128]{1,0:T(8,128)(2,1)} %get-tuple-element.6.rows_hbm, bf16[1024,512]{1,0:T(8,128)(2,1)} %get-tuple-element.7.parts_hbm), custom_call_target="tpu_custom_call" | custom-call | tf_op jit(solution)/shard_map/results/pallas_call | solution.py:604
